TPU v7x, 128 devices: a whole 4x4x4 slice. The times are simulated.
128 devices in a mesh: tiles: 128 (over y, x, z, core).
Axes of the slice: x: 4, y: 4, z: 4, core: 2. Of those that a mesh axis runs over, the one named last changes fastest.
Arguments:
- obs_feat: bfloat16 [262144, 256], P('tiles'), may hold values from -6 to 6
- obs_coords: float32 [3, 262144], P(None, 'tiles'), may hold values from -1 to 1
- send_rows: int32 [128, 128, 16], P('tiles'), may hold values from 0 to 2047, as said below
- send_count: int32 [128, 128], P('tiles'), may hold values from 8 to 16, as said below
- tile_id: int32 [128], P('tiles'), may hold values from 0 to 127, as said below
- cotangent: bfloat16 [524288, 512], P('tiles'), may hold values from -48 to 48
- projection: bfloat16 [256, 512], replicated, may hold values from -0.375 to 0.375
Outputs:
- grad_obs: bfloat16 [262144, 256], P('tiles')
- grad_weight: float32 [256, 512], replicated
- grad_gain: float32 [512], replicated
Inputs may be any that keep to these rules, and one draw needn't show every extreme that they name: `send_rows`: entries are local rows of owner s. No row is named twice in one device's block; a row is named by at most two slots in all, and then both are live and the second lies in the block of the device whose tile is the east neighbour of the first one's tile. `send_count`: some devices hold dense tiles whose count is 16 from every owner. `tile_id`: A permutation of the tiles.
All inputs are finite; a program needn't handle non-finite values.
Results may differ from a plain program's by a relative error of at most 0.0063.
Values may be sent and summed in bfloat16 or wider, within the bound.
No kernel may reach another device: no remote copies, remote signals or barrier semaphores. Data moves between devices by JAX's collectives and lax.ppermute only.
A program may use at most 64 MiB of HBM per device.

v0:
```python
import math

import jax
import jax.numpy as jnp
from jax import lax
from jax.sharding import PartitionSpec as P

TILE_LAT = 64
TILE_LON = 64


def cell_vectors(tile):
    lat_block = (tile // 16).astype(jnp.float32)
    lon_block = (tile % 16).astype(jnp.float32)
    row_pos = jnp.arange(TILE_LAT, dtype=jnp.float32)
    col_pos = jnp.arange(TILE_LON, dtype=jnp.float32)
    lat = (60.0 - (lat_block * TILE_LAT + row_pos + 0.5) * 0.25) * (math.pi / 180.0)
    lon = (-120.0 + (lon_block * TILE_LON + col_pos + 0.5) * 0.25) * (math.pi / 180.0)
    lat_all = jnp.broadcast_to(lat[:, None], (TILE_LAT, TILE_LON)).reshape(-1)
    lon_all = jnp.broadcast_to(lon[None, :], (TILE_LAT, TILE_LON)).reshape(-1)
    return jnp.stack(
        [jnp.cos(lat_all) * jnp.cos(lon_all), jnp.cos(lat_all) * jnp.sin(lon_all), jnp.sin(lat_all)]
    )


def tile_grad(cell_vecs, positions, grad_out):
    inv_width = 1.0 / (2.0 * (0.375 * math.pi / 180.0) ** 2)
    cells = cell_vecs.shape[1]
    block_len = min(cells, 1024)
    count_blocks = cells // block_len
    vec_blocks = cell_vecs.reshape(3, count_blocks, block_len).transpose(1, 0, 2)
    out_blocks = grad_out.reshape(count_blocks, block_len, grad_out.shape[1])
    channels = grad_out.shape[1]
    slots = positions.shape[1]

    def one_block(carry, pieces):
        acc_gain, acc_adj = carry
        vecs, grads = pieces
        dist = (vecs[0][:, None] - positions[0][None, :]) ** 2
        dist = dist + (vecs[1][:, None] - positions[1][None, :]) ** 2
        dist = dist + (vecs[2][:, None] - positions[2][None, :]) ** 2
        kernel = jnp.exp(-dist * inv_width)
        density = jnp.sum(kernel, axis=1)
        kernel_low = kernel.astype(jnp.bfloat16)
        weighted = (grads / (1.0 + density)[:, None]).astype(jnp.bfloat16)
        acc_gain = acc_gain + jnp.sum(jnp.log1p(density)[:, None] * grads, axis=0)
        acc_adj = acc_adj + lax.dot_general(
            kernel_low, weighted, (((0,), (0,)), ((), ())), preferred_element_type=jnp.float32
        )
        return ((acc_gain, acc_adj), None)

    start = (jnp.zeros((channels,), jnp.float32), jnp.zeros((slots, channels), jnp.float32))
    result, _ = lax.scan(one_block, start, (vec_blocks, out_blocks))
    return result


def shards(obs_feat, obs_coords, send_rows, send_count, tile_id, cotangent, projection):
    slot_rows = send_rows[0]
    counts = send_count[0]
    owners, slot_cap = slot_rows.shape
    feat_width = obs_feat.shape[1]
    live_mask = jnp.arange(slot_cap, dtype=jnp.int32)[None, :] < counts[:, None]
    flat_rows = slot_rows.reshape(-1)
    outgoing = jnp.where(
        live_mask[:, :, None],
        obs_feat[flat_rows].reshape(owners, slot_cap, feat_width),
        jnp.zeros((), jnp.bfloat16),
    )
    out_pos = obs_coords[:, flat_rows].reshape(3, owners, slot_cap).transpose(1, 0, 2)
    out_pos = jnp.where(live_mask[:, None, :], out_pos, jnp.zeros((), jnp.float32))
    in_pos = lax.all_to_all(out_pos, "tiles", split_axis=0, concat_axis=0, tiled=True)
    positions = in_pos.transpose(1, 0, 2).reshape(3, owners * slot_cap)
    part_gain, adjoint_sum = tile_grad(cell_vectors(tile_id[0]), positions, cotangent)
    adjoint = adjoint_sum.astype(jnp.bfloat16)
    incoming = lax.all_to_all(outgoing, "tiles", split_axis=0, concat_axis=0, tiled=True)
    features = incoming.reshape(owners * slot_cap, feat_width)
    part_weight = lax.dot_general(
        features, adjoint, (((0,), (0,)), ((), ())), preferred_element_type=jnp.float32
    )
    slot_grad = lax.dot_general(
        adjoint, projection, (((1,), (1,)), ((), ())), preferred_element_type=jnp.float32
    ).astype(jnp.bfloat16)
    returning = lax.all_to_all(
        slot_grad.reshape(owners, slot_cap, feat_width),
        "tiles",
        split_axis=0,
        concat_axis=0,
        tiled=True,
    )
    values = jnp.where(live_mask[:, :, None], returning, jnp.zeros((), jnp.bfloat16)).reshape(
        owners * slot_cap, feat_width
    )
    grad_obs = (
        jnp.zeros(obs_feat.shape, jnp.float32)
        .at[flat_rows]
        .add(values.astype(jnp.float32))
        .astype(jnp.bfloat16)
    )
    scaled_weight = part_weight * (1.0 / 256.0)
    scaled_gain = part_gain * (1.0 / 2048.0)
    grad_weight, grad_gain = lax.psum((scaled_weight, scaled_gain), "tiles")
    return (grad_obs, grad_weight, grad_gain)


def solution(mesh):
    return jax.shard_map(
        shards,
        mesh=mesh,
        in_specs=(
            P("tiles", None),
            P(None, "tiles"),
            P("tiles", None, None),
            P("tiles", None),
            P("tiles"),
            P("tiles", None),
            P(),
        ),
        out_specs=(P("tiles", None), P(), P()),
        check_vma=False,
    )
```

profile of v0, /device:TPU:1, one launch (start us, length us, event | category | flops | bytes accessed | tf_op | source)
XLA Modules:
  0.0 300.6 jit_solution(7974933575901998124)
XLA Ops:
  7.2 0.0 copy-start
  7.2 0.9 copy.19
  8.1 0.1 reshape_squeeze.3
  8.2 1.1 copy.20
  9.3 5.5 %gather_fusion = f32[2048,3]{1,0:T(8,128)S(1)} fusion(f32[3,2048]{0,1:T(8,128)S(1)} %copy.20, s32[2048]{0:T(1024)S(1)} %broadcast_clamp_fusion), kind=kCustom, calls=%fused_computation | custom fusion | bytes 57344 | tf_op jit(solution)/shard_map/gather | solution.py:69
  14.8 0.8 copy.21
  15.6 0.8 iota_compare_fusion
  16.4 0.8 select_bitcast_fusion
  17.2 11.5 %all-to-all-start = ((f32[128,3,16]{2,1,0:T(4,128)}), f32[128,3,16]{2,1,0:T(4,128)S(1)}, u32[]{:S(2)}, u32[]{:S(2)}) async-start(f32[128,3,16]{2,1,0:T(4,128)} %select_bitcast_fusion), calls=%async_computation | async-start | bytes 524288 | tf_op jit(solution)/shard_map/all_to_all | solution.py:71
  29.4 0.1 fusion.28
  29.4 0.1 cos.34
  29.5 0.1 sin.26
  29.6 0.1 fusion.26
  29.6 0.1 broadcast_in_dim.70
  29.7 0.1 cos.32
  29.8 0.1 broadcast_in_dim.75
  29.9 0.1 sin.28
  30.1 9.5 %all-to-all-done = f32[128,3,16]{2,1,0:T(4,128)S(1)} async-done(((f32[128,3,16]{2,1,0:T(4,128)}), f32[128,3,16]{2,1,0:T(4,128)S(1)}, u32[]{:S(2)}, u32[]{:S(2)}) %all-to-all-start) | async-done | bytes 24608 | tf_op jit(solution)/shard_map/all_to_all | solution.py:71
  39.6 0.1 reshape.235
  39.7 0.0 copy-start.2
  39.7 56.5 %while.13 = (s32[]{:T(128)}, f32[512]{0:T(512)S(1)}, f32[2048,512]{1,0:T(8,128)}, f32[4,3,1024]{2,1,0:T(4,128)S(1)}, f32[3,2048]{1,0:T(4,128)S(1)}, /*index=5*/b...) while((s32[]{:T(128)}, f32[512]{0:T(512)S(1)}, f32[2048,512]{1,0:T(8,128)}, ...), condition=%wide.region_3.4_spmd.clone, body=%wide.region_0.3_spmd.clone.sunk | while | flops 2198864384 | bytes 10666648 | solution.py:53
  39.8 3.6 %fusion.41 = f32[1024]{0:T(1024)S(1)} fusion(f32[2048]{0:T(1024)S(1)} %bitcast.60, f32[1024]{0:T(1024)S(1)} %bitcast.68, f32[2048]{0:T(1024)S(1)} %bitcast.62, f32[1024]{0:T(1024)S(1)} %bitcast.66, f32[2048]{0:T(1024)S(1)} %bitcast.58, f32[1024]{0:T(1024)S(1)} %bitcast.64), kind=kLoop, calls=%fused_computation.5.clone.1 | loop fusion | flops 23067648 | bytes 40960 | tf_op jit(solution)/shard_map/while/body/eval_jaxpr/reduce_sum | solution.py:43
  43.4 7.9 %select_add_fusion.5 = f32[2048,512]{1,0:T(8,128)} fusion(f32[2048,512]{1,0:T(8,128)} %get-tuple-element.152, f32[2048]{0:T(1024)S(1)} %bitcast.61, f32[1024]{0:T(1024)S(1)} %bitcast.69, f32[2048]{0:T(1024)S(1)} %bitcast.63, f32[1024]{0:T(1024)S(1)} %bitcast.67, f32[2048]{0:T(1024)S(1)} %bitcast.59, f32[1024]{0:T(1024)S(1)} %bitcast.65, ...), kind=kOutput, calls=%fused_computation.7.clone.1 | convolution fusion | flops 2174222336 | bytes 9478657 | tf_op jit(solution)/shard_map/while/body/eval_jaxpr/dot_general | solution.py:47
  51.4 1.5 fusion.42
  53.0 3.6 %fusion.41 = f32[1024]{0:T(1024)S(1)} fusion(f32[2048]{0:T(1024)S(1)} %bitcast.60, f32[1024]{0:T(1024)S(1)} %bitcast.68, f32[2048]{0:T(1024)S(1)} %bitcast.62, f32[1024]{0:T(1024)S(1)} %bitcast.66, f32[2048]{0:T(1024)S(1)} %bitcast.58, f32[1024]{0:T(1024)S(1)} %bitcast.64), kind=kLoop, calls=%fused_computation.5.clone.1 | loop fusion | flops 23067648 | bytes 40960 | tf_op jit(solution)/shard_map/while/body/eval_jaxpr/reduce_sum | solution.py:43
  56.6 9.2 %select_add_fusion.5 = f32[2048,512]{1,0:T(8,128)} fusion(f32[2048,512]{1,0:T(8,128)} %get-tuple-element.152, f32[2048]{0:T(1024)S(1)} %bitcast.61, f32[1024]{0:T(1024)S(1)} %bitcast.69, f32[2048]{0:T(1024)S(1)} %bitcast.63, f32[1024]{0:T(1024)S(1)} %bitcast.67, f32[2048]{0:T(1024)S(1)} %bitcast.59, f32[1024]{0:T(1024)S(1)} %bitcast.65, ...), kind=kOutput, calls=%fused_computation.7.clone.1 | convolution fusion | flops 2174222336 | bytes 9478657 | tf_op jit(solution)/shard_map/while/body/eval_jaxpr/dot_general | solution.py:47
  65.8 1.5 fusion.42
  67.4 3.6 %fusion.41 = f32[1024]{0:T(1024)S(1)} fusion(f32[2048]{0:T(1024)S(1)} %bitcast.60, f32[1024]{0:T(1024)S(1)} %bitcast.68, f32[2048]{0:T(1024)S(1)} %bitcast.62, f32[1024]{0:T(1024)S(1)} %bitcast.66, f32[2048]{0:T(1024)S(1)} %bitcast.58, f32[1024]{0:T(1024)S(1)} %bitcast.64), kind=kLoop, calls=%fused_computation.5.clone.1 | loop fusion | flops 23067648 | bytes 40960 | tf_op jit(solution)/shard_map/while/body/eval_jaxpr/reduce_sum | solution.py:43
  71.1 9.2 %select_add_fusion.5 = f32[2048,512]{1,0:T(8,128)} fusion(f32[2048,512]{1,0:T(8,128)} %get-tuple-element.152, f32[2048]{0:T(1024)S(1)} %bitcast.61, f32[1024]{0:T(1024)S(1)} %bitcast.69, f32[2048]{0:T(1024)S(1)} %bitcast.63, f32[1024]{0:T(1024)S(1)} %bitcast.67, f32[2048]{0:T(1024)S(1)} %bitcast.59, f32[1024]{0:T(1024)S(1)} %bitcast.65, ...), kind=kOutput, calls=%fused_computation.7.clone.1 | convolution fusion | flops 2174222336 | bytes 9478657 | tf_op jit(solution)/shard_map/while/body/eval_jaxpr/dot_general | solution.py:47
  80.3 1.5 fusion.42
  81.9 3.6 %fusion.41 = f32[1024]{0:T(1024)S(1)} fusion(f32[2048]{0:T(1024)S(1)} %bitcast.60, f32[1024]{0:T(1024)S(1)} %bitcast.68, f32[2048]{0:T(1024)S(1)} %bitcast.62, f32[1024]{0:T(1024)S(1)} %bitcast.66, f32[2048]{0:T(1024)S(1)} %bitcast.58, f32[1024]{0:T(1024)S(1)} %bitcast.64), kind=kLoop, calls=%fused_computation.5.clone.1 | loop fusion | flops 23067648 | bytes 40960 | tf_op jit(solution)/shard_map/while/body/eval_jaxpr/reduce_sum | solution.py:43
  85.5 9.2 %select_add_fusion.5 = f32[2048,512]{1,0:T(8,128)} fusion(f32[2048,512]{1,0:T(8,128)} %get-tuple-element.152, f32[2048]{0:T(1024)S(1)} %bitcast.61, f32[1024]{0:T(1024)S(1)} %bitcast.69, f32[2048]{0:T(1024)S(1)} %bitcast.63, f32[1024]{0:T(1024)S(1)} %bitcast.67, f32[2048]{0:T(1024)S(1)} %bitcast.59, f32[1024]{0:T(1024)S(1)} %bitcast.65, ...), kind=kOutput, calls=%fused_computation.7.clone.1 | convolution fusion | flops 2174222336 | bytes 9478657 | tf_op jit(solution)/shard_map/while/body/eval_jaxpr/dot_general | solution.py:47
  94.7 1.5 fusion.42
  96.3 0.0 copy-done.2
  96.3 3.9 %convolution_convert_fusion = bf16[2048,256]{1,0:T(8,128)(2,1)} fusion(bf16[256,512]{1,0:T(8,128)(2,1)S(1)} %copy-done.2, f32[2048,512]{1,0:T(8,128)} %get-tuple-element.36), kind=kOutput, calls=%fused_computation.29 | convolution fusion | flops 538443776 | bytes 5505024 | tf_op jit(solution)/shard_map/dot_general | solution.py:80
  100.2 4.5 %all-to-all-start.1 = ((bf16[128,16,256]{2,1,0:T(8,128)(2,1)}), bf16[128,16,256]{2,1,0:T(8,128)(2,1)S(1)}, u32[]{:S(2)}, u32[]{:S(2)}) async-start(bf16[128,16,256]{2,1,0:T(8,128)(2,1)} %bitcast.9), calls=%async_computation.1 | async-start | bytes 2097152 | tf_op jit(solution)/shard_map/all_to_all | solution.py:83
  104.7 0.0 all-reduce.2.cloned.1.call-start
  104.8 0.0 copy-done
  104.8 7.5 %gather_fusion.1 = bf16[2048,256]{1,0:T(8,128)(2,1)S(1)} fusion(bf16[2048,256]{1,0:T(8,128)(2,1)S(1)} %copy-done, s32[2048]{0:T(1024)S(1)} %broadcast_clamp_fusion), kind=kCustom, calls=%fused_computation.1 | custom fusion | bytes 2105344 | tf_op jit(solution)/shard_map/gather | solution.py:66
  112.3 11.7 %all-to-all-done.1 = bf16[128,16,256]{2,1,0:T(8,128)(2,1)S(1)} async-done(((bf16[128,16,256]{2,1,0:T(8,128)(2,1)}), bf16[128,16,256]{2,1,0:T(8,128)(2,1)S(1)}, u32[]{:S(2)}, u32[]{:S(2)}) %all-to-all-start.1) | async-done | bytes 1048608 | tf_op jit(solution)/shard_map/all_to_all | solution.py:83
  124.0 0.0 copy-start.1
  124.0 1.2 broadcast_select_fusion
  125.2 23.4 %all_to_all.15 = bf16[128,16,256]{2,1,0:T(8,128)(2,1)S(1)} all-to-all(bf16[128,16,256]{2,1,0:T(8,128)(2,1)S(1)} %get-tuple-element.79), channel_id=1, replica_groups=mesh['tiles'=128] {'tiles'}, dimensions={0} | all-to-all | bytes 2097152 | tf_op jit(solution)/shard_map/all_to_all | solution.py:75
  148.6 0.0 copy-done.1
  148.6 1.5 convolution_multiply_fusion
  150.2 0.0 all-reduce.2.cloned.1.call-update
  150.2 63.0 %psum.15 = f32[512]{0:T(512)} all-reduce(f32[512]{0:T(512)S(1)} %broadcast_multiply_fusion.2), channel_id=1, replica_groups=mesh['tiles'=128] {'tiles'}, use_global_device_ids=true, to_apply=%region_6.7 | all-reduce | flops 512 | bytes 4096 | tf_op jit(solution)/shard_map/psum | solution.py:101
  213.2 11.4 %scatter_custom_fusion = f32[2048,256]{1,0:T(8,128)S(1)} fusion(s32[2048]{0:T(1024)S(1)} %bitcast.71, bf16[2048,256]{1,0:T(8,128)(2,1)} %bitcast.53, f32[]{:T(128)} %constant.28.clone.1), kind=kCustom, calls=%fused_computation.30 | custom fusion | flops 1048576 | bytes 3145732 | tf_op jit(solution)/shard_map/scatter-add | solution.py:96
  224.7 1.1 convert_element_type.40
  225.7 66.1 %all-reduce.2.cloned.1.call-done = f32[256,512]{1,0:T(8,128)} async-done(((f32[256,512]{1,0:T(8,128)}), f32[256,512]{1,0:T(8,128)}) %all-reduce.2.cloned.1.call-update) | async-done | bytes 524304 | tf_op jit(solution)/shard_map/psum | solution.py:101
  291.8 1.9 copy.34
  (26 shorter events, 0.4 us)
Async XLA Ops:
  7.2 97.6 %copy-start = (bf16[2048,256]{1,0:T(8,128)(2,1)S(1)}, bf16[2048,256]{1,0:T(8,128)(2,1)}, u32[]{:S(2)}) copy-start(bf16[2048,256]{1,0:T(8,128)(2,1)} %param.9) | copy-start | bytes 3145732
  17.2 22.4 %all-to-all-start = ((f32[128,3,16]{2,1,0:T(4,128)}), f32[128,3,16]{2,1,0:T(4,128)S(1)}, u32[]{:S(2)}, u32[]{:S(2)}) async-start(f32[128,3,16]{2,1,0:T(4,128)} %select_bitcast_fusion), calls=%async_computation | async-start | bytes 524288 | tf_op jit(solution)/shard_map/all_to_all | solution.py:71
  39.7 56.5 %copy-start.2 = (bf16[256,512]{1,0:T(8,128)(2,1)S(1)}, bf16[256,512]{1,0:T(8,128)(2,1)}, u32[]{:S(2)}) copy-start(bf16[256,512]{1,0:T(8,128)(2,1)} %param.15) | copy-start | bytes 786436
  100.2 23.8 %all-to-all-start.1 = ((bf16[128,16,256]{2,1,0:T(8,128)(2,1)}), bf16[128,16,256]{2,1,0:T(8,128)(2,1)S(1)}, u32[]{:S(2)}, u32[]{:S(2)}) async-start(bf16[128,16,256]{2,1,0:T(8,128)(2,1)} %bitcast.9), calls=%async_computation.1 | async-start | bytes 2097152 | tf_op jit(solution)/shard_map/all_to_all | solution.py:83
  104.7 187.1 %all-reduce.2.cloned.1.call-start = ((), (), s32[]{:S(2)}) async-start(), calls=%async_computation.3 | async-start | bytes 1048576 | tf_op jit(solution)/shard_map/psum | solution.py:101
  124.0 24.6 %copy-start.1 = (f32[2048,512]{1,0:T(8,128)S(1)}, f32[2048,512]{1,0:T(8,128)}, u32[]{:S(2)}) copy-start(f32[2048,512]{1,0:T(8,128)} %get-tuple-element.36) | copy-start | bytes 12582916
Sparse Core Ops, SparseCore 0:
  150.3 141.4 all-reduce.1
where the time goes:
time: 301 us
  waiting for transfers between devices  87.3 us (29%)
  blocking collectives  86.4 us (29%)
  matrix products  41 us (14%)
  other arithmetic  36.1 us (12%)
  local copies, waits for them, and re-layouts  18.6 us (6%)
  starting transfers between devices  16.1 us (5%)
  between operations  14.9 us (5%)
    psum x1, waiting for transfers between devices, shards(): grad_weight, grad_gain = lax.psum((scaled_weight, scaled_gain), 'tiles')  66.1 us
    psum x1, blocking collectives, shards(): grad_weight, grad_gain = lax.psum((scaled_weight, scaled_gain), 'tiles')  63 us
    dot_general x4, matrix products, one_block(): lax.dot_general(kernel_low, weighted, (((0,), (0,)), ((), ())), preferred...  35.6 us
    all_to_all x1, blocking collectives, shards(): lax.all_to_all(outgoing, 'tiles', split_axis=0, concat_axis=0, tiled=True)  23.4 us
    reduce_sum x4, other arithmetic, one_block(): density = jnp.sum(kernel, axis=1)  14.5 us
    all_to_all x1, waiting for transfers between devices, shards(): lax.all_to_all(slot_grad.reshape(owners, slot_cap, feat_width), 'tiles',...  11.7 us
    all_to_all x1, starting transfers between devices, shards(): lax.all_to_all(out_pos, 'tiles', split_axis=0, concat_axis=0, tiled=True)  11.5 us
    scatter-add x1, other arithmetic, shards(): grad_obs = jnp.zeros(obs_feat.shape, jnp.float32).at[flat_rows].add(value...  11.4 us
  transfers between devices with their start and end apart: 3, of which 3 were waited for; matrix products, arithmetic and copies ran while one was open for 7% of the time, Pallas kernels for 0%

commit v1 on v0

v1 whole, which is shorter than its diff:
```python
import functools
import math

import jax
import jax.numpy as jnp
from jax import lax
from jax.experimental import pallas as pl
from jax.experimental.pallas import tpu as pltpu
from jax.sharding import PartitionSpec as P

f32, bf16 = jnp.float32, jnp.bfloat16
N_DEV = 128
CAP = 16
SLOTS = 2048
ROWS = 2048
FEAT = 256
CHAN = 512
CELLS = 4096
KAPPA = 1.0 / (2.0 * (0.375 * math.pi / 180.0) ** 2) / math.log(2.0)
VM = pl.BlockSpec(memory_space=pltpu.VMEM)


def call(body, out_shape, n_in, scratch=(), in_specs=None, name=None, limit=56, cost=None):
    many = isinstance(out_shape, (tuple, list))
    return pl.pallas_call(
        body,
        out_shape=out_shape,
        in_specs=in_specs or [VM] * n_in,
        out_specs=tuple(VM for _ in out_shape) if many else VM,
        scratch_shapes=list(scratch),
        compiler_params=pltpu.CompilerParams(vmem_limit_bytes=limit * 1024 * 1024),
        name=name,
        cost_estimate=cost,
    )


def cost(flops, nbytes):
    return pl.CostEstimate(flops=flops, bytes_accessed=nbytes, transcendentals=0)


def gather_pos(rl_ref, coords_ref, out_ref):
    x = coords_ref[...]
    hi = x.astype(bf16).astype(f32)
    mid = (x - hi).astype(bf16).astype(f32)
    lo = (x - hi) - mid
    parts = jnp.concatenate([hi, mid, lo, jnp.zeros((7, ROWS), f32)], axis=0).astype(bf16)
    for b in range(SLOTS // 256):
        acc = jnp.zeros((16, 256), f32)
        hot = []
        for h in range(2):
            row = rl_ref[2 * b + h : 2 * b + h + 1, :]
            iota = lax.broadcasted_iota(jnp.int32, (ROWS, 128), 0)
            hot.append(jnp.where(iota == row, 1.0, 0.0).astype(bf16))
        acc = jnp.dot(parts, jnp.concatenate(hot, axis=1), preferred_element_type=f32)
        pos = (acc[0:3] + acc[3:6]) + acc[6:9]
        for h in range(2):
            out_ref[:, 2 * b + h : 2 * b + h + 1, :] = pos[:, 128 * h : 128 * h + 128].reshape(3, 1, 128)


def gather_feat(rl_ref, feat_ref, out_ref, hot_ref):
    for b in range(4):
        for q in range(4):
            r = 4 * b + q
            col = jnp.broadcast_to(rl_ref[r : r + 1, :].astype(f32), (128, 128)).T
            lane = lax.broadcasted_iota(jnp.int32, (128, 128), 1).astype(f32)
            for t in range(ROWS // 128):
                hot_ref[128 * q : 128 * q + 128, 128 * t : 128 * t + 128] = jnp.where(
                    col - 128.0 * t == lane, 1.0, 0.0
                ).astype(bf16)
        out_ref[512 * b : 512 * b + 512, :] = jnp.dot(
            hot_ref[...], feat_ref[...], preferred_element_type=f32
        ).astype(bf16)


def adjoint_kernel(pos_ref, trig_ref, cott_ref, adjt_ref, gain_ref, v_ref, m_ref, k_ref, w_ref, dens_ref):
    cl, sl = trig_ref[0], trig_ref[1]
    cp, sp = trig_ref[2], trig_ref[3]
    for b in range(16):
        px, py, pz = pos_ref[0, b : b + 1, :], pos_ref[1, b : b + 1, :], pos_ref[2, b : b + 1, :]
        r2 = px * px + py * py
        inv = lax.rsqrt(jnp.maximum(r2, 1e-30))
        rho = r2 * inv
        cs = slice(128 * b, 128 * b + 128)
        v_ref[:, cs] = (-KAPPA * rho) * ((cl - px * inv) ** 2 + (sl - py * inv) ** 2)
        m_ref[:, cs] = -KAPPA * ((cp - rho) ** 2 + (sp - pz) ** 2)

    def group(g, _):
        base = pl.multiple_of(g * 8, 8)
        cc = trig_ref[2, pl.ds(base, 8), :]
        rows = []
        for m in range(4):
            ds = []
            for h in range(2):
                i = 2 * m + h
                c = cc[i : i + 1, :]
                d = jnp.zeros((64, 128), f32)
                for b in range(16):
                    cs = slice(128 * b, 128 * b + 128)
                    mm = m_ref[pl.ds(base, 8), cs]
                    k = jnp.exp2(c * v_ref[:, cs] + mm[i : i + 1, :])
                    d = d + k
                    k_ref[pl.ds(pl.multiple_of(g * 512, 512) + 64 * i, 64), cs] = k.astype(bf16)
                ds.append(d)
            rows.append(jnp.sum(jnp.concatenate(ds, axis=0).T, axis=0, keepdims=True))
        dens_ref[g] = jnp.concatenate(rows, axis=0)
        return 0

    lax.fori_loop(0, 8, group, 0)
    dens = dens_ref[...].reshape(32, 128)
    scale = 1.0 / (1.0 + dens)
    logd = jnp.log1p(dens)
    for r in range(4):
        rs = slice(128 * r, 128 * r + 128)
        g = jnp.zeros((128, 128), f32)
        for t in range(32):
            cs = slice(128 * t, 128 * t + 128)
            x = cott_ref[rs, cs].astype(f32)
            w_ref[rs, cs] = (x * scale[t : t + 1, :]).astype(bf16)
            g = g + x * logd[t : t + 1, :]
        gain_ref[r : r + 1, :] = jnp.sum(g.T, axis=0, keepdims=True) * (1.0 / 2048.0)

    def cols(n, _):
        cs = pl.ds(pl.multiple_of(n * 512, 512), 512)
        adjt_ref[:, cs] = jnp.dot(w_ref[...], k_ref[:, cs], preferred_element_type=f32).astype(bf16)
        return 0

    lax.fori_loop(0, SLOTS // 512, cols, 0)


def finish_tile(adjt_ref, feat_ref, proj_ref, out_ref):
    for n in range(SLOTS // 512):
        s = jnp.dot(proj_ref[...], adjt_ref[:, 512 * n : 512 * n + 512], preferred_element_type=f32)
        for h in range(2):
            t = s[128 * h : 128 * h + 128, :].T.astype(bf16)
            out_ref[8 * n : 8 * n + 8, :, 16 * h : 16 * h + 16, :] = t.reshape(8, 4, 16, 128)
    w = jnp.dot(adjt_ref[...], feat_ref[...], preferred_element_type=f32) * (1.0 / 256.0)
    for cb in range(4):
        wt = w[128 * cb : 128 * cb + 128, :].T.astype(bf16)
        out_ref[:, cb, 32:40, :] = wt.reshape(32, 8, 128)


def reduce_block(recv_ref, gain_ref, out_ref):
    total = jnp.sum(recv_ref[:, 32:40, :].astype(f32), axis=0)
    g = gain_ref[...]
    hi = g.astype(bf16).astype(f32)
    block = jnp.concatenate([total, hi, g - hi], axis=0).astype(bf16)
    out_ref[...] = jnp.broadcast_to(block[None], (N_DEV, 16, 128))


def scatter_rows(rl_ref, recv_ref, out_ref, val_ref, hot_ref):
    for h in range(2):
        val_ref[:, 128 * h : 128 * h + 128] = recv_ref[:, 16 * h : 16 * h + 16, :].reshape(SLOTS, 128)

    def rows(n, _):
        iota = lax.broadcasted_iota(jnp.int32, (512, 128), 0) + n * 512
        for b in range(16):
            hot_ref[:, 128 * b : 128 * b + 128] = jnp.where(iota == rl_ref[b : b + 1, :], 1.0, 0.0).astype(bf16)
        out_ref[pl.ds(pl.multiple_of(n * 512, 512), 512), :] = jnp.dot(
            hot_ref[...], val_ref[...], preferred_element_type=f32
        ).astype(bf16)
        return 0

    lax.fori_loop(0, ROWS // 512, rows, 0)


def assemble(x_ref, weight_ref, gain_ref):
    total = jnp.zeros((8, 128), f32)
    for cb in range(4):
        x = x_ref[:, cb].astype(f32)
        weight_ref[:, 128 * cb : 128 * cb + 128] = x[:, 0:8, :].reshape(256, 128)
        total = total + jnp.sum(x[:, 8:16, :], axis=0)
    gain_ref[...] = total[0:4] + total[4:8]


def trig_tables(tile):
    step = jnp.arange(64, dtype=f32)
    lat = (60.0 - ((tile // 16).astype(f32) * 64 + step + 0.5) * 0.25) * (math.pi / 180.0)
    lon = (-120.0 + ((tile % 16).astype(f32) * 64 + step + 0.5) * 0.25) * (math.pi / 180.0)
    t = jnp.stack([jnp.cos(lon), jnp.sin(lon), jnp.cos(lat), jnp.sin(lat)])
    return jnp.broadcast_to(t[:, :, None], (4, 64, 128))


def exchange(x):
    return lax.all_to_all(x, "tiles", split_axis=0, concat_axis=0, tiled=True)


def shards(obs_feat, obs_coords, send_rows, send_count, tile_id, cotangent, projection):
    sds = jax.ShapeDtypeStruct
    live = jnp.arange(CAP, dtype=jnp.int32)[None, :] < send_count[0][:, None]
    rl = jnp.where(live, send_rows[0], -1).reshape(16, 128)

    pos_out = call(gather_pos, sds((3, 16, 128), f32), 2, name="gather_pos")(rl, obs_coords)
    pos_out = pos_out.reshape(3, N_DEV, CAP).transpose(1, 0, 2).reshape(N_DEV, 1, 48)
    pos_out = jnp.pad(pos_out, ((0, 0), (0, 0), (0, 80)))
    pos_in = exchange(pos_out)[:, 0, :48]
    pos = pos_in.reshape(N_DEV, 3, CAP).transpose(1, 0, 2).reshape(3, 16, 128)

    feat_out = call(
        gather_feat, sds((SLOTS, FEAT), bf16), 2, scratch=[pltpu.VMEM((512, ROWS), bf16)], name="gather_feat",
        cost=cost(4 * 10**9, 2 * 2**20),
    )(rl, obs_feat)
    cott = cotangent.T
    trig = trig_tables(tile_id[0])

    feat_in = exchange(feat_out.reshape(N_DEV, CAP, FEAT)).reshape(SLOTS, FEAT)
    adjt, gain = call(
        adjoint_kernel,
        (sds((CHAN, SLOTS), bf16), sds((4, 128), f32)),
        3,
        scratch=[
            pltpu.VMEM((64, SLOTS), f32),
            pltpu.VMEM((64, SLOTS), f32),
            pltpu.VMEM((CELLS, SLOTS), bf16),
            pltpu.VMEM((CHAN, CELLS), bf16),
            pltpu.VMEM((8, 4, 128), f32),
        ],
        name="adjoint",
        cost=cost(20 * 10**9, 8 * 2**20),
    )(pos, trig, cott)

    out = call(finish_tile, sds((32, 4, 40, 128), bf16), 3, name="finish_tile")(adjt, feat_in, projection)
    recv = exchange(out.reshape(N_DEV, 40, 128))
    block = call(reduce_block, sds((N_DEV, 16, 128), bf16), 2, name="reduce_block")(recv, gain)
    blocks = exchange(block)
    grad_obs = call(
        scatter_rows,
        sds((ROWS, FEAT), bf16),
        2,
        scratch=[pltpu.VMEM((SLOTS, FEAT), bf16), pltpu.VMEM((512, SLOTS), bf16)],
        name="scatter_rows",
        cost=cost(4 * 10**9, 3 * 2**20),
    )(rl, recv)
    weight, gain_sum = call(
        assemble, (sds((FEAT, CHAN), f32), sds((4, 128), f32)), 1, name="assemble"
    )(blocks.reshape(32, 4, 16, 128))
    return grad_obs, weight, gain_sum.reshape(CHAN)


def solution(mesh):
    return jax.shard_map(
        shards,
        mesh=mesh,
        in_specs=(
            P("tiles", None),
            P(None, "tiles"),
            P("tiles", None, None),
            P("tiles", None),
            P("tiles"),
            P("tiles", None),
            P(),
        ),
        out_specs=(P("tiles", None), P(), P()),
        check_vma=False,
    )
```

time: 301 us -> 128 us (0.43)
  waiting for transfers between devices: 87.3 us -> 8.17 us
  blocking collectives: 86.4 us -> 31.8 us
  Pallas kernels: 0 us -> 45 us
  matrix products: 41 us -> 0 us
  other arithmetic: 36.1 us -> 2.04 us
  between operations: 14.9 us -> 1.4 us
  starting transfers between devices: 16.1 us -> 25.9 us
  local copies, waits for them, and re-layouts: 18.6 us -> 13.3 us
    psum x1 -> x0, waiting for transfers between devices: 66.1 us -> none  [shards(): grad_weight, grad_gain = lax.psum((scaled_weight, scaled_gain), 'tiles')]
    psum x1 -> x0, blocking collectives: 63 us -> none  [shards(): grad_weight, grad_gain = lax.psum((scaled_weight, scaled_gain), 'tiles')]
    pallas_call x0 -> x7, Pallas kernels: none -> 45 us  [the longest x1 22 us: shards(): call(adjoint_kernel, (sds((CHAN, SLOTS), bf16), sds((4, 128), f32)), 3, s...]
    dot_general x6 -> x0, matrix products: 41 us -> none  [the longest x4 35.6 us: one_block(): lax.dot_general(kernel_low, weighted, (((0,), (0,)), ((), ())), preferred...]
    reduce_sum x8 -> x0, other arithmetic: 20.5 us -> none  [the longest x4 14.5 us: one_block(): density = jnp.sum(kernel, axis=1)]
    all_to_all x2 -> x3, waiting for transfers between devices: 21.2 us -> 8.17 us  [exchange(): return lax.all_to_all(x, 'tiles', split_axis=0, concat_axis=0, tiled=True)]
    gather x2 -> x0, local copies, waits for them, and re-layouts: 13 us -> none  [the longest x1 7.5 us: shards(): obs_feat[flat_rows].reshape(owners, slot_cap, feat_width)]
    scatter-add x1 -> x0, other arithmetic: 11.4 us -> none  [shards(): grad_obs = jnp.zeros(obs_feat.shape, jnp.float32).at[flat_rows].add(value...]
  transfers between devices with their start and end apart: 3 -> 3, of which waited for: 3 -> 1; matrix products, arithmetic and copies ran while one was open for 7% -> 6% of each run, Pallas kernels for 0% -> 27%
where the time goes in v1:
time: 128 us
  Pallas kernels  45 us (35%)
  blocking collectives  31.8 us (25%)
  starting transfers between devices  25.9 us (20%)
  local copies, waits for them, and re-layouts  13.3 us (10%)
  waiting for transfers between devices  8.17 us (6%)
  other arithmetic  2.04 us (2%)
  between operations  1.4 us (1%)
    all_to_all x1, blocking collectives, exchange(): return lax.all_to_all(x, 'tiles', split_axis=0, concat_axis=0, tiled=True)  31.8 us
    all_to_all x3, starting transfers between devices, exchange(): return lax.all_to_all(x, 'tiles', split_axis=0, concat_axis=0, tiled=True)  25.9 us
    pallas_call x1, Pallas kernels, shards(): call(adjoint_kernel, (sds((CHAN, SLOTS), bf16), sds((4, 128), f32)), 3, s...  22 us
    unnamed x9, local copies, waits for them, and re-layouts  9.66 us
    all_to_all x3, waiting for transfers between devices, exchange(): return lax.all_to_all(x, 'tiles', split_axis=0, concat_axis=0, tiled=True)  8.17 us
    pallas_call x1, Pallas kernels, shards(): call(gather_feat, sds((SLOTS, FEAT), bf16), 2, scratch=[pltpu.VMEM((512,...  6.34 us
    pallas_call x1, Pallas kernels, shards(): call(scatter_rows, sds((ROWS, FEAT), bf16), 2, scratch=[pltpu.VMEM((SLOTS...  5.55 us
    pallas_call x1, Pallas kernels, shards(): call(finish_tile, sds((32, 4, 40, 128), bf16), 3, name='finish_tile')  4.33 us
  transfers between devices with their start and end apart: 3, of which 1 were waited for; matrix products, arithmetic and copies ran while one was open for 6% of the time, Pallas kernels for 27%

profile of v1, /device:TPU:1, one launch (start us, length us, event | category | flops | bytes accessed | tf_op | source)
XLA Modules:
  0.0 127.6 jit_solution(13983462714531016856)
XLA Ops:
  0.6 0.5 broadcast.164
  1.1 1.3 %reduce.3 = s32[128]{0:T(128)S(1)} reduce(s32[1,128]{1,0:T(1,128)} %param.10, s32[]{:T(128)} %broadcast.164), dimensions={0}, to_apply=%param.10.reduce_sub_computation.3 | reduce | bytes 1028 | tf_op args[3]
  2.5 0.1 lt.31
  2.5 0.1 lt.32
  2.6 0.1 lt.33
  2.7 0.8 copy.16
  3.5 0.1 squeeze.6
  3.6 0.1 lt.29
  3.7 0.6 compare_select_fusion.rl_ref
  4.3 2.6 %gather_pos.1 = f32[3,16,128]{2,1,0:T(8,128)} custom-call(s32[16,128]{1,0:T(8,128)} %compare_select_fusion.rl_ref, f32[3,2048]{1,0:T(4,128)} %coords_ref.1), custom_call_target="tpu_custom_call" | custom-call | tf_op jit(solution)/shard_map/gather_pos/pallas_call | solution.py:192
  6.9 0.8 reshape.90
  7.8 0.1 copy.17
  7.8 0.1 copy.23
  8.0 0.7 pad.4.clone
  8.6 11.5 %all-to-all-start = ((f32[128,1,128]{2,1,0:T(1,128)}), f32[128,1,128]{2,1,0:T(1,128)S(1)}, u32[]{:S(2)}, u32[]{:S(2)}) async-start(f32[128,1,128]{2,1,0:T(1,128)} %pad.4.clone), calls=%async_computation | async-start | bytes 131072 | tf_op jit(solution)/shard_map/all_to_all | solution.py:184
  20.8 0.1 fusion.2
  20.9 0.1 fusion
  20.9 6.4 %copy.21 = bf16[4096,512]{0,1:T(8,128)(2,1)} copy(bf16[4096,512]{1,0:T(8,128)(2,1)} %param.12) | data formatting | bytes 8388608 | tf_op args[5]
  27.4 6.3 %gather_feat.1 = bf16[2048,256]{1,0:T(8,128)(2,1)} custom-call(s32[16,128]{1,0:T(8,128)} %compare_select_fusion.rl_ref, bf16[2048,256]{1,0:T(8,128)(2,1)} %feat_ref.1), custom_call_target="tpu_custom_call" | custom-call | flops 4000000000 | bytes 2097152 | tf_op jit(solution)/shard_map/gather_feat/pallas_call | solution.py:198
  33.7 0.0 all-to-all-done
  33.7 9.8 %all-to-all-start.1 = ((bf16[128,16,256]{2,1,0:T(8,128)(2,1)}), bf16[128,16,256]{2,1,0:T(8,128)(2,1)S(1)}, u32[]{:S(2)}, u32[]{:S(2)}) async-start(bf16[128,16,256]{2,1,0:T(8,128)(2,1)} %bitcast.21), calls=%async_computation.1 | async-start | bytes 2097152 | tf_op jit(solution)/shard_map/all_to_all | solution.py:184
  43.5 0.1 copy.22
  43.5 0.1 copy.20
  43.7 0.7 reshape.92.pos_ref
  44.4 0.8 broadcast_in_dim.12.trig_ref
  45.2 22.0 %adjoint.1 = (bf16[512,2048]{1,0:T(8,128)(2,1)}, f32[4,128]{1,0:T(4,128)}) custom-call(f32[3,16,128]{2,1,0:T(8,128)} %reshape.92.pos_ref, f32[4,64,128]{2,1,0:T(8,128)} %broadcast_in_dim.12.trig_ref, bf16[512,4096]{1,0:T(8,128)(2,1)} %bitcast.18), custom_call_target="tpu_custom_call" | custom-call | flops 20000000000 | bytes 8388608 | tf_op jit(solution)/shard_map/adjoint/pallas_call | solution.py:206
  67.1 0.0 all-to-all-done.1
  67.1 0.0 copy-start
  67.1 1.0 copy-done
  68.1 4.3 %finish_tile.1 = bf16[32,4,40,128]{3,2,1,0:T(8,128)(2,1)} custom-call(bf16[512,2048]{1,0:T(8,128)(2,1)} %get-tuple-element.7.adjt_ref, bf16[2048,256]{1,0:T(8,128)(2,1)} %bitcast.19, bf16[256,512]{1,0:T(8,128)(2,1)} %proj_ref.1), custom_call_target="tpu_custom_call" | custom-call | tf_op jit(solution)/shard_map/finish_tile/pallas_call | solution.py:221
  72.4 31.8 %all_to_all.20.recv_ref = bf16[128,40,128]{2,1,0:T(8,128)(2,1)} all-to-all(bf16[128,40,128]{2,1,0:T(8,128)(2,1)} %bitcast.17), channel_id=1, replica_groups=mesh['tiles'=128] {'tiles'}, dimensions={0} | all-to-all | bytes 2621440 | tf_op jit(solution)/shard_map/all_to_all | solution.py:184
  104.2 2.3 %reduce_block.1 = bf16[128,16,128]{2,1,0:T(8,128)(2,1)} custom-call(bf16[128,40,128]{2,1,0:T(8,128)(2,1)} %all_to_all.20.recv_ref, f32[4,128]{1,0:T(4,128)} %get-tuple-element.8.gain_ref), custom_call_target="tpu_custom_call" | custom-call | tf_op jit(solution)/shard_map/reduce_block/pallas_call | solution.py:223
  106.5 4.6 %all-to-all-start.3 = ((bf16[128,16,128]{2,1,0:T(8,128)(2,1)}), bf16[128,16,128]{2,1,0:T(8,128)(2,1)S(1)}, u32[]{:S(2)}, u32[]{:S(2)}) async-start(bf16[128,16,128]{2,1,0:T(8,128)(2,1)} %reduce_block.1), calls=%async_computation.3 | async-start | bytes 1048576 | tf_op jit(solution)/shard_map/all_to_all | solution.py:184
  111.2 5.5 %scatter_rows.1 = bf16[2048,256]{1,0:T(8,128)(2,1)} custom-call(s32[16,128]{1,0:T(8,128)} %compare_select_fusion.rl_ref, bf16[128,40,128]{2,1,0:T(8,128)(2,1)} %all_to_all.20.recv_ref), custom_call_target="tpu_custom_call" | custom-call | flops 4000000000 | bytes 3145728 | tf_op jit(solution)/shard_map/scatter_rows/pallas_call | solution.py:225
  116.7 8.2 %all-to-all-done.3 = bf16[128,16,128]{2,1,0:T(8,128)(2,1)S(1)} async-done(((bf16[128,16,128]{2,1,0:T(8,128)(2,1)}), bf16[128,16,128]{2,1,0:T(8,128)(2,1)S(1)}, u32[]{:S(2)}, u32[]{:S(2)}) %all-to-all-start.3) | async-done | bytes 524320 | tf_op jit(solution)/shard_map/all_to_all | solution.py:184
  124.9 0.0 copy-start.1
  124.9 0.8 copy-done.1
  125.7 1.9 %assemble.1 = (f32[256,512]{1,0:T(8,128)}, f32[4,128]{1,0:T(4,128)}) custom-call(bf16[32,4,16,128]{3,2,1,0:T(8,128)(2,1)} %bitcast.20), custom_call_target="tpu_custom_call" | custom-call | tf_op jit(solution)/shard_map/assemble/pallas_call | solution.py:233
  (2 shorter events, 0.0 us)
Async XLA Ops:
  8.6 25.1 %all-to-all-start = ((f32[128,1,128]{2,1,0:T(1,128)}), f32[128,1,128]{2,1,0:T(1,128)S(1)}, u32[]{:S(2)}, u32[]{:S(2)}) async-start(f32[128,1,128]{2,1,0:T(1,128)} %pad.4.clone), calls=%async_computation | async-start | bytes 131072 | tf_op jit(solution)/shard_map/all_to_all | solution.py:184
  33.7 33.4 %all-to-all-start.1 = ((bf16[128,16,256]{2,1,0:T(8,128)(2,1)}), bf16[128,16,256]{2,1,0:T(8,128)(2,1)S(1)}, u32[]{:S(2)}, u32[]{:S(2)}) async-start(bf16[128,16,256]{2,1,0:T(8,128)(2,1)} %bitcast.21), calls=%async_computation.1 | async-start | bytes 2097152 | tf_op jit(solution)/shard_map/all_to_all | solution.py:184
  67.1 1.0 copy-start
  106.5 18.4 %all-to-all-start.3 = ((bf16[128,16,128]{2,1,0:T(8,128)(2,1)}), bf16[128,16,128]{2,1,0:T(8,128)(2,1)S(1)}, u32[]{:S(2)}, u32[]{:S(2)}) async-start(bf16[128,16,128]{2,1,0:T(8,128)(2,1)} %reduce_block.1), calls=%async_computation.3 | async-start | bytes 1048576 | tf_op jit(solution)/shard_map/all_to_all | solution.py:184
  124.9 0.8 copy-start.1

commit v2 on v1

v2 whole, which is shorter than its diff:
```python
import functools
import math

import jax
import jax.numpy as jnp
from jax import lax
from jax.experimental import pallas as pl
from jax.experimental.pallas import tpu as pltpu
from jax.sharding import PartitionSpec as P

f32, bf16 = jnp.float32, jnp.bfloat16
N_DEV = 128
CAP = 16
SLOTS = 2048
ROWS = 2048
FEAT = 256
CHAN = 512
CELLS = 4096
KAPPA = 1.0 / (2.0 * (0.375 * math.pi / 180.0) ** 2) / math.log(2.0)
VM = pl.BlockSpec(memory_space=pltpu.VMEM)


def call(body, out_shape, n_in, scratch=(), in_specs=None, name=None, limit=56, cost=None):
    many = isinstance(out_shape, (tuple, list))
    return pl.pallas_call(
        body,
        out_shape=out_shape,
        in_specs=in_specs or [VM] * n_in,
        out_specs=tuple(VM for _ in out_shape) if many else VM,
        scratch_shapes=list(scratch),
        compiler_params=pltpu.CompilerParams(vmem_limit_bytes=limit * 1024 * 1024),
        name=name,
        cost_estimate=cost,
    )


def cost(flops, nbytes):
    return pl.CostEstimate(flops=flops, bytes_accessed=nbytes, transcendentals=0)


def slot_major(x):
    lane = lax.broadcasted_iota(jnp.int32, (128, 128), 1) // 16
    sub = lax.broadcasted_iota(jnp.int32, (128, 128), 0) % 8
    y = jnp.where(lane == sub, jnp.concatenate([x] * 8, axis=1), jnp.zeros((), x.dtype))
    return jnp.sum(y.reshape(16, 8, 128), axis=1)


def gather_pos(rows_ref, count_ref, coords_ref, out_ref):
    slot = lax.broadcasted_iota(jnp.int32, (16, 128), 0)
    rows = jnp.where(slot < count_ref[...], rows_ref[...], -1)
    block, lane = rows >> 7, rows & 127
    pos = [jnp.zeros((16, 128), f32) for _ in range(3)]
    for t in range(ROWS // 128):
        hit = block == t
        for c in range(3):
            src = jnp.broadcast_to(coords_ref[c : c + 1, 128 * t : 128 * t + 128], (16, 128))
            got = jnp.take_along_axis(src, lane, axis=1, mode="promise_in_bounds")
            pos[c] = jnp.where(hit, got, pos[c])
    out_ref[...] = jnp.concatenate(pos + [jnp.zeros((80, 128), f32)], axis=0).T


def gather_feat(rows_ref, feat_ref, out_ref, rl_ref, hot_ref):
    x = jnp.concatenate([rows_ref[...].astype(f32), jnp.zeros((112, 128), f32)], axis=0).T
    rl = slot_major(x[:, 0:16])
    rl_ref[...] = rl.astype(jnp.int32)
    lane = lax.broadcasted_iota(jnp.int32, (128, 128), 1)
    for b in range(4):
        for q in range(4):
            r = 4 * b + q
            col = jnp.broadcast_to(rl[r : r + 1, :], (128, 128)).T.astype(jnp.int32)
            for t in range(ROWS // 128):
                hot_ref[128 * q : 128 * q + 128, 128 * t : 128 * t + 128] = jnp.where(
                    col == lane + 128 * t, 1.0, 0.0
                ).astype(bf16)
        out_ref[512 * b : 512 * b + 512, :] = jnp.dot(
            hot_ref[...], feat_ref[...], preferred_element_type=f32
        ).astype(bf16)


def adjoint_kernel(
    recv_ref, trig_ref, cot_hbm, adj_ref, gain_ref, c_ref, v_ref, m_ref, k_ref, w_ref, dens_ref, cot_ref, gacc_ref, sem
):
    load = pltpu.make_async_copy(cot_hbm, cot_ref, sem)
    load.start()
    cl, sl, cp, sp = [jnp.broadcast_to(trig_ref[:, i : i + 1], (64, 128)) for i in range(4)]
    c_ref[...] = cp
    x, y, z = [slot_major(recv_ref[:, 16 * c : 16 * c + 16]) for c in range(3)]
    for b in range(16):
        px, py, pz = x[b : b + 1, :], y[b : b + 1, :], z[b : b + 1, :]
        r2 = px * px + py * py
        inv = lax.rsqrt(jnp.maximum(r2, 1e-30))
        rho = r2 * inv
        cs = slice(128 * b, 128 * b + 128)
        v_ref[:, cs] = (-KAPPA * rho) * ((cl - px * inv) ** 2 + (sl - py * inv) ** 2)
        m_ref[:, cs] = -KAPPA * ((cp - rho) ** 2 + (sp - pz) ** 2)

    def group(g, _):
        base = pl.multiple_of(g * 8, 8)
        cc = c_ref[pl.ds(base, 8), :]
        rows = []
        for m in range(4):
            ds = []
            for h in range(2):
                i = 2 * m + h
                c = cc[i : i + 1, :]
                d = jnp.zeros((64, 128), f32)
                for b in range(16):
                    cs = slice(128 * b, 128 * b + 128)
                    mm = m_ref[pl.ds(base, 8), cs]
                    k = jnp.exp2(c * v_ref[:, cs] + mm[i : i + 1, :])
                    d = d + k
                    k_ref[pl.ds(pl.multiple_of(g * 512, 512) + 64 * i, 64), cs] = k.astype(bf16)
                ds.append(d)
            rows.append(jnp.sum(jnp.concatenate(ds, axis=0).T, axis=0, keepdims=True))
        dens_ref[g] = jnp.concatenate(rows, axis=0)
        return 0

    lax.fori_loop(0, 8, group, 0)
    load.wait()
    gacc_ref[...] = jnp.zeros_like(gacc_ref)

    def weigh(g, _):
        dens = dens_ref[g]
        scale = 1.0 / (1.0 + dens)
        logd = jnp.log1p(dens)
        for m in range(4):
            rs = pl.ds(pl.multiple_of(g * 512 + 128 * m, 128), 128)
            sc = jnp.broadcast_to(scale[m : m + 1, :], (128, 128)).T
            lg = jnp.broadcast_to(logd[m : m + 1, :], (128, 128)).T
            for q in range(4):
                cs = slice(128 * q, 128 * q + 128)
                x = cot_ref[rs, cs].astype(f32)
                w_ref[rs, cs] = (x * sc).astype(bf16)
                gacc_ref[:, cs] += jnp.sum((x * lg).reshape(16, 8, 128), axis=0)
        return 0

    lax.fori_loop(0, 8, weigh, 0)
    gain_ref[...] = jnp.sum(gacc_ref[...], axis=0, keepdims=True) * (1.0 / 2048.0)

    def slots(n, _):
        rs = pl.ds(pl.multiple_of(n * 512, 512), 512)
        adj_ref[rs, :] = lax.dot_general(
            k_ref[:, rs], w_ref[...], (((0,), (0,)), ((), ())), preferred_element_type=f32
        ).astype(bf16)
        return 0

    lax.fori_loop(0, SLOTS // 512, slots, 0)


def finish_tile(adj_ref, feat_ref, proj_ref, out_ref):
    for n in range(SLOTS // 512):
        s = lax.dot_general(
            adj_ref[512 * n : 512 * n + 512, :], proj_ref[...], (((1,), (1,)), ((), ())), preferred_element_type=f32
        ).astype(bf16)
        for h in range(2):
            t = s[:, 128 * h : 128 * h + 128]
            out_ref[8 * n : 8 * n + 8, :, 2 * h : 2 * h + 2] = t.reshape(8, 4, 2, 8, 128)
    w = lax.dot_general(feat_ref[...], adj_ref[...], (((0,), (0,)), ((), ())), preferred_element_type=f32)
    w = (w * (1.0 / 256.0)).astype(bf16)
    for cb in range(4):
        out_ref[:, cb, 4] = w[:, 128 * cb : 128 * cb + 128].reshape(32, 8, 128)


def reduce_block(recv_ref, gain_ref, out_ref):
    total = jnp.sum(recv_ref[:, 0].astype(f32), axis=0)
    g = jnp.concatenate([gain_ref[:, 128 * i : 128 * i + 128] for i in range(4)], axis=0)
    hi = g.astype(bf16).astype(f32)
    block = jnp.stack([total, jnp.concatenate([hi, g - hi], axis=0)]).astype(bf16)
    out_ref[...] = jnp.broadcast_to(block[None], (N_DEV, 2, 8, 128))


def scatter_rows(rl_ref, recv_ref, out_ref, val_ref, hot_ref):
    for h in range(2):
        val_ref[:, 128 * h : 128 * h + 128] = recv_ref[:, 2 * h : 2 * h + 2].reshape(SLOTS, 128)

    def rows(n, _):
        iota = lax.broadcasted_iota(jnp.int32, (512, 128), 0) + n * 512
        for b in range(16):
            hot_ref[:, 128 * b : 128 * b + 128] = jnp.where(iota == rl_ref[b : b + 1, :], 1.0, 0.0).astype(bf16)
        out_ref[pl.ds(pl.multiple_of(n * 512, 512), 512), :] = jnp.dot(
            hot_ref[...], val_ref[...], preferred_element_type=f32
        ).astype(bf16)
        return 0

    lax.fori_loop(0, ROWS // 512, rows, 0)


def assemble(x_ref, weight_ref, gain_ref):
    total = jnp.zeros((8, 128), f32)
    for cb in range(4):
        weight_ref[:, 128 * cb : 128 * cb + 128] = x_ref[:, cb, 0].astype(f32).reshape(256, 128)
        total = total + jnp.sum(x_ref[:, cb, 1].astype(f32), axis=0)
    gain_ref[...] = total[0:4] + total[4:8]


def trig_tables(tile):
    step = jnp.arange(64, dtype=f32)
    lat = (60.0 - ((tile // 16).astype(f32) * 64 + step + 0.5) * 0.25) * (math.pi / 180.0)
    lon = (-120.0 + ((tile % 16).astype(f32) * 64 + step + 0.5) * 0.25) * (math.pi / 180.0)
    return jnp.stack([jnp.cos(lon), jnp.sin(lon), jnp.cos(lat), jnp.sin(lat)], axis=1)


def exchange(x):
    return lax.all_to_all(x, "tiles", split_axis=0, concat_axis=0, tiled=True)


def shards(obs_feat, obs_coords, send_rows, send_count, tile_id, cotangent, projection):
    sds = jax.ShapeDtypeStruct
    rows = send_rows[0].T
    msg = call(gather_pos, sds((N_DEV, 128), f32), 3, name="gather_pos", limit=8)(rows, send_count, obs_coords)
    pos_in = exchange(msg.reshape(N_DEV, 1, 128)).reshape(N_DEV, 128)

    feat_out, rl = call(
        gather_feat,
        (sds((SLOTS, FEAT), bf16), sds((16, 128), jnp.int32)),
        2,
        scratch=[pltpu.VMEM((512, ROWS), bf16)],
        name="gather_feat",
        limit=16,
        cost=cost(4 * 10**9, 2 * 2**20),
    )(rows, obs_feat)
    trig = trig_tables(tile_id[0])

    feat_in = exchange(feat_out.reshape(N_DEV, CAP, FEAT)).reshape(SLOTS, FEAT)
    adj, gain = call(
        adjoint_kernel,
        (sds((SLOTS, CHAN), bf16), sds((1, CHAN), f32)),
        3,
        in_specs=[VM, VM, pl.BlockSpec(memory_space=pl.ANY)],
        scratch=[
            pltpu.VMEM((64, 128), f32),
            pltpu.VMEM((64, SLOTS), f32),
            pltpu.VMEM((64, SLOTS), f32),
            pltpu.VMEM((CELLS, SLOTS), bf16),
            pltpu.VMEM((CELLS, CHAN), bf16),
            pltpu.VMEM((8, 4, 128), f32),
            pltpu.VMEM((CELLS, CHAN), bf16),
            pltpu.VMEM((8, CHAN), f32),
            pltpu.SemaphoreType.DMA,
        ],
        name="adjoint",
        limit=48,
        cost=cost(20 * 10**9, 8 * 2**20),
    )(pos_in, trig, cotangent)

    out = call(finish_tile, sds((32, 4, 5, 8, 128), bf16), 3, name="finish_tile", limit=24)(adj, feat_in, projection)
    recv = exchange(out.reshape(N_DEV, 5, 8, 128))
    block = pl.pallas_call(
        reduce_block,
        grid=(1,),
        out_shape=sds((N_DEV, 2, 8, 128), bf16),
        in_specs=[pl.BlockSpec((N_DEV, 1, 8, 128), lambda i: (0, 4, 0, 0)), pl.BlockSpec((1, CHAN), lambda i: (0, 0))],
        out_specs=pl.BlockSpec((N_DEV, 2, 8, 128), lambda i: (0, 0, 0, 0)),
        name="reduce_block",
    )(recv, gain)
    blocks = exchange(block)
    grad_obs = call(
        scatter_rows,
        sds((ROWS, FEAT), bf16),
        2,
        scratch=[pltpu.VMEM((SLOTS, FEAT), bf16), pltpu.VMEM((512, SLOTS), bf16)],
        name="scatter_rows",
        limit=16,
        cost=cost(4 * 10**9, 3 * 2**20),
    )(rl, recv)
    weight, gain_sum = call(
        assemble, (sds((FEAT, CHAN), f32), sds((4, 128), f32)), 1, name="assemble", limit=8
    )(blocks.reshape(32, 4, 2, 8, 128))
    return grad_obs, weight, gain_sum.reshape(CHAN)


def solution(mesh):
    return jax.shard_map(
        shards,
        mesh=mesh,
        in_specs=(
            P("tiles", None),
            P(None, "tiles"),
            P("tiles", None, None),
            P("tiles", None),
            P("tiles"),
            P("tiles", None),
            P(),
        ),
        out_specs=(P("tiles", None), P(), P()),
        check_vma=False,
    )
```

time: 128 us -> 107 us (0.84)
  Pallas kernels: 45 us -> 32.8 us
  local copies, waits for them, and re-layouts: 13.3 us -> 4.7 us
  waiting for transfers between devices: 8.17 us -> 11.1 us
  other arithmetic: 2.04 us -> 0.11 us
  starting transfers between devices: 25.9 us -> 24.3 us
    pallas_call x5, Pallas kernels: 37.5 us -> 27.8 us  [the longest x1 18.6 us: shards(): call(adjoint_kernel, (sds((SLOTS, CHAN), bf16), sds((1, CHAN), f32)), 3,...]
    unnamed x9 -> x16, local copies, waits for them, and re-layouts: 9.66 us -> 4.6 us
    all_to_all x3, waiting for transfers between devices: 8.17 us -> 11.1 us  [exchange(): return lax.all_to_all(x, 'tiles', split_axis=0, concat_axis=0, tiled=True)]
    all_to_all x3, starting transfers between devices: 25.9 us -> 24.3 us  [exchange(): return lax.all_to_all(x, 'tiles', split_axis=0, concat_axis=0, tiled=True)]
    reshape x2 -> x0, local copies, waits for them, and re-layouts: 1.56 us -> none  [the longest x1 0.84 us: shards(): pos_out.reshape(3, N_DEV, CAP).transpose(1, 0, 2).reshape(N_DEV, 1, 48)]
    pallas_call x1, Pallas kernels: 5.55 us -> 4.21 us  [shards(): call(scatter_rows, sds((ROWS, FEAT), bf16), 2, scratch=[pltpu.VMEM((SLOTS...]
    unnamed x1 -> x0, other arithmetic: 1.32 us -> none
  transfers between devices with their start and end apart: 3 -> 3, of which waited for: 1 -> 2; matrix products, arithmetic and copies ran while one was open for 6% -> 0% of each run, Pallas kernels for 27% -> 26%
where the time goes in v2:
time: 107 us; the launch traced here: 106 us
  Pallas kernels  32.8 us (31%)
  blocking collectives  31.6 us (30%)
  starting transfers between devices  24.3 us (23%)
  waiting for transfers between devices  11.1 us (10%)
  local copies, waits for them, and re-layouts  4.7 us (4%)
  between operations  1.4 us (1%)
    all_to_all x1, blocking collectives, exchange(): return lax.all_to_all(x, 'tiles', split_axis=0, concat_axis=0, tiled=True)  31.6 us
    all_to_all x3, starting transfers between devices, exchange(): return lax.all_to_all(x, 'tiles', split_axis=0, concat_axis=0, tiled=True)  24.3 us
    pallas_call x1, Pallas kernels, shards(): call(adjoint_kernel, (sds((SLOTS, CHAN), bf16), sds((1, CHAN), f32)), 3,...  18.6 us
    all_to_all x3, waiting for transfers between devices, exchange(): return lax.all_to_all(x, 'tiles', split_axis=0, concat_axis=0, tiled=True)  11.1 us
    pallas_call x1, Pallas kernels, shards(): call(gather_feat, (sds((SLOTS, FEAT), bf16), sds((16, 128), jnp.int32)),...  4.92 us
    unnamed x16, local copies, waits for them, and re-layouts  4.6 us
    pallas_call x1, Pallas kernels, shards(): call(scatter_rows, sds((ROWS, FEAT), bf16), 2, scratch=[pltpu.VMEM((SLOTS...  4.21 us
  transfers between devices with their start and end apart: 3, of which 2 were waited for; matrix products, arithmetic and copies ran while one was open for 0% of the time, Pallas kernels for 26%

profile of v2, /device:TPU:1, one launch (start us, length us, event | category | flops | bytes accessed | tf_op | source)
XLA Modules:
  0.0 106.0 jit_solution(9393090625482499026)
XLA Ops:
  0.6 0.0 copy-start.2
  0.6 0.7 copy-done.2
  1.4 0.0 copy-start.3
  1.4 0.7 copy-done.3
  2.1 0.0 copy-start.6
  2.1 0.7 copy-done.6
  2.7 0.9 gather_pos.1
  3.7 11.5 %all-to-all-start = ((f32[128,1,128]{2,1,0:T(1,128)}), f32[128,1,128]{2,1,0:T(1,128)S(1)}, u32[]{:S(2)}, u32[]{:S(2)}) async-start(f32[128,1,128]{2,1,0:T(1,128)} %bitcast.4), calls=%async_computation | async-start | bytes 131072 | tf_op jit(solution)/shard_map/all_to_all | solution.py:204
  15.8 0.1 fusion.2
  15.9 0.1 fusion
  15.9 0.0 copy-start.4
  16.0 0.7 copy-done.4
  16.7 0.0 copy-start.7
  16.7 1.2 %copy-done.7 = bf16[2048,256]{1,0:T(8,128)(2,1)S(1)} copy-done((bf16[2048,256]{1,0:T(8,128)(2,1)S(1)}, bf16[2048,256]{1,0:T(8,128)(2,1)}, u32[]{:S(2)}) %copy-start.7) | copy-done | bytes 1048600
  17.9 4.9 %gather_feat.1 = (bf16[2048,256]{1,0:T(8,128)(2,1)}, s32[16,128]{1,0:T(8,128)S(1)}) custom-call(s32[16,128]{1,0:T(8,128)S(1)} %bitcast.22, bf16[2048,256]{1,0:T(8,128)(2,1)S(1)} %copy-done.7), custom_call_target="tpu_custom_call" | custom-call | flops 4000000000 | bytes 2097152 | tf_op jit(solution)/shard_map/gather_feat/pallas_call | solution.py:213
  22.8 0.1 copy.11.trig_ref
  22.9 1.6 %all-to-all-done = f32[128,1,128]{2,1,0:T(1,128)S(1)} async-done(((f32[128,1,128]{2,1,0:T(1,128)}), f32[128,1,128]{2,1,0:T(1,128)S(1)}, u32[]{:S(2)}, u32[]{:S(2)}) %all-to-all-start) | async-done | bytes 65568 | tf_op jit(solution)/shard_map/all_to_all | solution.py:204
  24.5 8.2 %all-to-all-start.1 = ((bf16[128,16,256]{2,1,0:T(8,128)(2,1)}), bf16[128,16,256]{2,1,0:T(8,128)(2,1)S(1)}, u32[]{:S(2)}, u32[]{:S(2)}) async-start(bf16[128,16,256]{2,1,0:T(8,128)(2,1)} %bitcast.7), calls=%async_computation.1 | async-start | bytes 2097152 | tf_op jit(solution)/shard_map/all_to_all | solution.py:204
  32.7 0.0 copy-start.1
  32.7 18.6 %adjoint.1 = (bf16[2048,512]{1,0:T(8,128)(2,1)S(1)}, f32[1,512]{1,0:T(1,128)S(1)}) custom-call(f32[128,128]{1,0:T(8,128)S(1)} %bitcast.20, f32[64,4]{1,0:T(8,128)S(1)} %copy.11.trig_ref, bf16[4096,512]{1,0:T(8,128)(2,1)} %cot_hbm.1), custom_call_target="tpu_custom_call" | custom-call | flops 20000000000 | bytes 8388608 | tf_op jit(solution)/shard_map/adjoint/pallas_call | solution.py:225
  51.3 0.0 copy-start.5
  51.4 0.6 copy-done.5
  51.9 0.0 all-to-all-done.1
  51.9 0.0 copy-done.1
  51.9 1.3 %finish_tile.1 = bf16[32,4,5,8,128]{4,3,2,1,0:T(8,128)(2,1)S(1)} custom-call(bf16[2048,512]{1,0:T(8,128)(2,1)S(1)} %get-tuple-element.10.adj_ref, bf16[2048,256]{1,0:T(8,128)(2,1)S(1)} %bitcast.18, bf16[256,512]{1,0:T(8,128)(2,1)S(1)} %copy-done.1), custom_call_target="tpu_custom_call" | custom-call | tf_op jit(solution)/shard_map/finish_tile/pallas_call | solution.py:246
  53.2 31.6 %all_to_all.20.recv_ref = bf16[128,5,8,128]{3,2,1,0:T(8,128)(2,1)} all-to-all(bf16[128,5,8,128]{3,2,1,0:T(8,128)(2,1)S(1)} %bitcast.17), channel_id=1, replica_groups=mesh['tiles'=128] {'tiles'}, dimensions={0} | all-to-all | bytes 2621440 | tf_op jit(solution)/shard_map/all_to_all | solution.py:204
  84.8 0.0 copy-start
  84.8 2.0 %reduce_block.1 = bf16[128,2,8,128]{3,2,1,0:T(8,128)(2,1)} custom-call(bf16[128,5,8,128]{3,2,1,0:T(8,128)(2,1)} %all_to_all.20.recv_ref, f32[1,512]{1,0:T(1,128)} %copy-done.5), custom_call_target="tpu_custom_call" | custom-call | tf_op jit(solution)/shard_map/reduce_block/pallas_call | solution.py:248
  86.8 4.6 %all-to-all-start.3 = ((bf16[128,2,8,128]{3,2,1,0:T(8,128)(2,1)}), bf16[128,2,8,128]{3,2,1,0:T(8,128)(2,1)S(1)}, u32[]{:S(2)}, u32[]{:S(2)}) async-start(bf16[128,2,8,128]{3,2,1,0:T(8,128)(2,1)} %reduce_block.1), calls=%async_computation.3 | async-start | bytes 1048576 | tf_op jit(solution)/shard_map/all_to_all | solution.py:204
  91.5 0.0 copy-done
  91.5 4.2 %scatter_rows.1 = bf16[2048,256]{1,0:T(8,128)(2,1)} custom-call(s32[16,128]{1,0:T(8,128)S(1)} %get-tuple-element.9.rl_ref, bf16[128,5,8,128]{3,2,1,0:T(8,128)(2,1)S(1)} %copy-done), custom_call_target="tpu_custom_call" | custom-call | flops 4000000000 | bytes 3145728 | tf_op jit(solution)/shard_map/scatter_rows/pallas_call | solution.py:257
  95.7 9.5 %all-to-all-done.3 = bf16[128,2,8,128]{3,2,1,0:T(8,128)(2,1)S(1)} async-done(((bf16[128,2,8,128]{3,2,1,0:T(8,128)(2,1)}), bf16[128,2,8,128]{3,2,1,0:T(8,128)(2,1)S(1)}, u32[]{:S(2)}, u32[]{:S(2)}) %all-to-all-start.3) | async-done | bytes 524320 | tf_op jit(solution)/shard_map/all_to_all | solution.py:204
  105.2 0.9 assemble.1
  (1 shorter events, 0.0 us)
Async XLA Ops:
  0.6 0.8 copy-start.2
  1.4 0.7 copy-start.3
  2.1 0.7 copy-start.6
  3.7 20.8 %all-to-all-start = ((f32[128,1,128]{2,1,0:T(1,128)}), f32[128,1,128]{2,1,0:T(1,128)S(1)}, u32[]{:S(2)}, u32[]{:S(2)}) async-start(f32[128,1,128]{2,1,0:T(1,128)} %bitcast.4), calls=%async_computation | async-start | bytes 131072 | tf_op jit(solution)/shard_map/all_to_all | solution.py:204
  15.9 0.7 copy-start.4
  16.7 1.2 %copy-start.7 = (bf16[2048,256]{1,0:T(8,128)(2,1)S(1)}, bf16[2048,256]{1,0:T(8,128)(2,1)}, u32[]{:S(2)}) copy-start(bf16[2048,256]{1,0:T(8,128)(2,1)} %feat_ref.1) | copy-start | bytes 3145732
  24.5 27.4 %all-to-all-start.1 = ((bf16[128,16,256]{2,1,0:T(8,128)(2,1)}), bf16[128,16,256]{2,1,0:T(8,128)(2,1)S(1)}, u32[]{:S(2)}, u32[]{:S(2)}) async-start(bf16[128,16,256]{2,1,0:T(8,128)(2,1)} %bitcast.7), calls=%async_computation.1 | async-start | bytes 2097152 | tf_op jit(solution)/shard_map/all_to_all | solution.py:204
  32.7 19.2 %copy-start.1 = (bf16[256,512]{1,0:T(8,128)(2,1)S(1)}, bf16[256,512]{1,0:T(8,128)(2,1)}, u32[]{:S(2)}) copy-start(bf16[256,512]{1,0:T(8,128)(2,1)} %proj_ref.1) | copy-start | bytes 786436
  51.3 0.6 copy-start.5
  84.8 6.7 %copy-start = (bf16[128,5,8,128]{3,2,1,0:T(8,128)(2,1)S(1)}, bf16[128,5,8,128]{3,2,1,0:T(8,128)(2,1)}, u32[]{:S(2)}) copy-start(bf16[128,5,8,128]{3,2,1,0:T(8,128)(2,1)} %all_to_all.20.recv_ref) | copy-start | bytes 3932164
  86.8 18.4 %all-to-all-start.3 = ((bf16[128,2,8,128]{3,2,1,0:T(8,128)(2,1)}), bf16[128,2,8,128]{3,2,1,0:T(8,128)(2,1)S(1)}, u32[]{:S(2)}, u32[]{:S(2)}) async-start(bf16[128,2,8,128]{3,2,1,0:T(8,128)(2,1)} %reduce_block.1), calls=%async_computation.3 | async-start | bytes 1048576 | tf_op jit(solution)/shard_map/all_to_all | solution.py:204

commit v3 on v2

--- a/solution.py
+++ b/solution.py
@@ -18,9 +18,11 @@
 CELLS = 4096
 KAPPA = 1.0 / (2.0 * (0.375 * math.pi / 180.0) ** 2) / math.log(2.0)
 VM = pl.BlockSpec(memory_space=pltpu.VMEM)
-
-
-def call(body, out_shape, n_in, scratch=(), in_specs=None, name=None, limit=56, cost=None):
+HBM = pl.BlockSpec(memory_space=pltpu.HBM)
+DMA = pltpu.SemaphoreType.DMA
+
+
+def call(body, out_shape, n_in, scratch=(), in_specs=None, name=None, limit=24, cost=None):
     many = isinstance(out_shape, (tuple, list))
     return pl.pallas_call(
         body,
@@ -28,7 +30,7 @@
         in_specs=in_specs or [VM] * n_in,
         out_specs=tuple(VM for _ in out_shape) if many else VM,
         scratch_shapes=list(scratch),
-        compiler_params=pltpu.CompilerParams(vmem_limit_bytes=limit * 1024 * 1024),
+        compiler_params=pltpu.CompilerParams(vmem_limit_bytes=int(limit * 1024 * 1024)),
         name=name,
         cost_estimate=cost,
     )
@@ -45,7 +47,16 @@
     return jnp.sum(y.reshape(16, 8, 128), axis=1)
 
 
-def gather_pos(rows_ref, count_ref, coords_ref, out_ref):
+def load_all(pairs, sems):
+    copies = [pltpu.make_async_copy(src, dst, sems.at[i]) for i, (src, dst) in enumerate(pairs)]
+    for c in copies:
+        c.start()
+    return copies
+
+
+def gather_pos(rows_hbm, count_hbm, coords_hbm, out_ref, rows_ref, count_ref, coords_ref, sems):
+    for c in load_all([(rows_hbm, rows_ref), (count_hbm, count_ref), (coords_hbm, coords_ref)], sems):
+        c.wait()
     slot = lax.broadcasted_iota(jnp.int32, (16, 128), 0)
     rows = jnp.where(slot < count_ref[...], rows_ref[...], -1)
     block, lane = rows >> 7, rows & 127
@@ -59,7 +70,9 @@
     out_ref[...] = jnp.concatenate(pos + [jnp.zeros((80, 128), f32)], axis=0).T
 
 
-def gather_feat(rows_ref, feat_ref, out_ref, rl_ref, hot_ref):
+def gather_feat(rows_hbm, feat_hbm, out_ref, rl_ref, hot_ref, rows_ref, feat_ref, sems):
+    loads = load_all([(rows_hbm, rows_ref), (feat_hbm, feat_ref)], sems)
+    loads[0].wait()
     x = jnp.concatenate([rows_ref[...].astype(f32), jnp.zeros((112, 128), f32)], axis=0).T
     rl = slot_major(x[:, 0:16])
     rl_ref[...] = rl.astype(jnp.int32)
@@ -72,6 +85,8 @@
                 hot_ref[128 * q : 128 * q + 128, 128 * t : 128 * t + 128] = jnp.where(
                     col == lane + 128 * t, 1.0, 0.0
                 ).astype(bf16)
+        if b == 0:
+            loads[1].wait()
         out_ref[512 * b : 512 * b + 512, :] = jnp.dot(
             hot_ref[...], feat_ref[...], preferred_element_type=f32
         ).astype(bf16)
@@ -138,16 +153,22 @@
     gain_ref[...] = jnp.sum(gacc_ref[...], axis=0, keepdims=True) * (1.0 / 2048.0)
 
     def slots(n, _):
-        rs = pl.ds(pl.multiple_of(n * 512, 512), 512)
+        rs = pl.ds(pl.multiple_of(n * 1024, 1024), 1024)
         adj_ref[rs, :] = lax.dot_general(
             k_ref[:, rs], w_ref[...], (((0,), (0,)), ((), ())), preferred_element_type=f32
         ).astype(bf16)
         return 0
 
-    lax.fori_loop(0, SLOTS // 512, slots, 0)
-
-
-def finish_tile(adj_ref, feat_ref, proj_ref, out_ref):
+    lax.fori_loop(0, SLOTS // 1024, slots, 0)
+
+
+def finish_tile(adj_ref, feat_ref, proj_hbm, out_ref, proj_ref, sems):
+    load = load_all([(proj_hbm, proj_ref)], sems)[0]
+    w = lax.dot_general(feat_ref[...], adj_ref[...], (((0,), (0,)), ((), ())), preferred_element_type=f32)
+    w = (w * (1.0 / 256.0)).astype(bf16)
+    for cb in range(4):
+        out_ref[:, cb, 4] = w[:, 128 * cb : 128 * cb + 128].reshape(32, 8, 128)
+    load.wait()
     for n in range(SLOTS // 512):
         s = lax.dot_general(
             adj_ref[512 * n : 512 * n + 512, :], proj_ref[...], (((1,), (1,)), ((), ())), preferred_element_type=f32
@@ -155,14 +176,10 @@
         for h in range(2):
             t = s[:, 128 * h : 128 * h + 128]
             out_ref[8 * n : 8 * n + 8, :, 2 * h : 2 * h + 2] = t.reshape(8, 4, 2, 8, 128)
-    w = lax.dot_general(feat_ref[...], adj_ref[...], (((0,), (0,)), ((), ())), preferred_element_type=f32)
-    w = (w * (1.0 / 256.0)).astype(bf16)
-    for cb in range(4):
-        out_ref[:, cb, 4] = w[:, 128 * cb : 128 * cb + 128].reshape(32, 8, 128)
 
 
 def reduce_block(recv_ref, gain_ref, out_ref):
-    total = jnp.sum(recv_ref[:, 0].astype(f32), axis=0)
+    total = jnp.sum(recv_ref[:, 4].astype(f32), axis=0)
     g = jnp.concatenate([gain_ref[:, 128 * i : 128 * i + 128] for i in range(4)], axis=0)
     hi = g.astype(bf16).astype(f32)
     block = jnp.stack([total, jnp.concatenate([hi, g - hi], axis=0)]).astype(bf16)
@@ -207,16 +224,25 @@
 def shards(obs_feat, obs_coords, send_rows, send_count, tile_id, cotangent, projection):
     sds = jax.ShapeDtypeStruct
     rows = send_rows[0].T
-    msg = call(gather_pos, sds((N_DEV, 128), f32), 3, name="gather_pos", limit=8)(rows, send_count, obs_coords)
+    msg = call(
+        gather_pos,
+        sds((N_DEV, 128), f32),
+        3,
+        in_specs=[HBM] * 3,
+        scratch=[pltpu.VMEM((CAP, N_DEV), jnp.int32), pltpu.VMEM((1, N_DEV), jnp.int32), pltpu.VMEM((3, ROWS), f32), DMA((3,))],
+        name="gather_pos",
+        limit=60.47,
+    )(rows, send_count, obs_coords)
     pos_in = exchange(msg.reshape(N_DEV, 1, 128)).reshape(N_DEV, 128)
 
     feat_out, rl = call(
         gather_feat,
         (sds((SLOTS, FEAT), bf16), sds((16, 128), jnp.int32)),
         2,
-        scratch=[pltpu.VMEM((512, ROWS), bf16)],
+        in_specs=[HBM] * 2,
+        scratch=[pltpu.VMEM((512, ROWS), bf16), pltpu.VMEM((CAP, N_DEV), jnp.int32), pltpu.VMEM((ROWS, FEAT), bf16), DMA((2,))],
         name="gather_feat",
-        limit=16,
+        limit=59,
         cost=cost(4 * 10**9, 2 * 2**20),
     )(rows, obs_feat)
     trig = trig_tables(tile_id[0])
@@ -226,7 +252,7 @@
         adjoint_kernel,
         (sds((SLOTS, CHAN), bf16), sds((1, CHAN), f32)),
         3,
-        in_specs=[VM, VM, pl.BlockSpec(memory_space=pl.ANY)],
+        in_specs=[VM, VM, HBM],
         scratch=[
             pltpu.VMEM((64, 128), f32),
             pltpu.VMEM((64, SLOTS), f32),
@@ -236,23 +262,24 @@
             pltpu.VMEM((8, 4, 128), f32),
             pltpu.VMEM((CELLS, CHAN), bf16),
             pltpu.VMEM((8, CHAN), f32),
-            pltpu.SemaphoreType.DMA,
+            DMA,
         ],
         name="adjoint",
         limit=48,
         cost=cost(20 * 10**9, 8 * 2**20),
     )(pos_in, trig, cotangent)
 
-    out = call(finish_tile, sds((32, 4, 5, 8, 128), bf16), 3, name="finish_tile", limit=24)(adj, feat_in, projection)
+    out = call(
+        finish_tile,
+        sds((32, 4, 5, 8, 128), bf16),
+        3,
+        in_specs=[VM, VM, HBM],
+        scratch=[pltpu.VMEM((FEAT, CHAN), bf16), DMA((1,))],
+        name="finish_tile",
+        limit=24,
+    )(adj, feat_in, projection)
     recv = exchange(out.reshape(N_DEV, 5, 8, 128))
-    block = pl.pallas_call(
-        reduce_block,
-        grid=(1,),
-        out_shape=sds((N_DEV, 2, 8, 128), bf16),
-        in_specs=[pl.BlockSpec((N_DEV, 1, 8, 128), lambda i: (0, 4, 0, 0)), pl.BlockSpec((1, CHAN), lambda i: (0, 0))],
-        out_specs=pl.BlockSpec((N_DEV, 2, 8, 128), lambda i: (0, 0, 0, 0)),
-        name="reduce_block",
-    )(recv, gain)
+    block = call(reduce_block, sds((N_DEV, 2, 8, 128), bf16), 2, name="reduce_block", limit=8)(recv, gain)
     blocks = exchange(block)
     grad_obs = call(
         scatter_rows,

time: 107 us -> 102 us (0.953)
  local copies, waits for them, and re-layouts: 4.7 us -> 0.11 us
  waiting for transfers between devices: 11.1 us -> 13.3 us
  starting transfers between devices: 24.3 us -> 23.1 us
    unnamed x16 -> x4, local copies, waits for them, and re-layouts: 4.6 us -> 0.01 us
    all_to_all x3, waiting for transfers between devices: 11.1 us -> 13.3 us  [exchange(): return lax.all_to_all(x, 'tiles', split_axis=0, concat_axis=0, tiled=True)]
    all_to_all x3, starting transfers between devices: 24.3 us -> 23.1 us  [exchange(): return lax.all_to_all(x, 'tiles', split_axis=0, concat_axis=0, tiled=True)]
  transfers between devices with their start and end apart: 3 -> 3, of which waited for: 2 -> 3; matrix products, arithmetic and copies ran while one was open for 0% -> 0% of each run, Pallas kernels for 26% -> 28%
where the time goes in v3:
time: 102 us
  Pallas kernels  33.1 us (32%)
  blocking collectives  30.6 us (30%)
  starting transfers between devices  23.1 us (23%)
  waiting for transfers between devices  13.3 us (13%)
  between operations  1.39 us (1%)
    all_to_all x1, blocking collectives, exchange(): return lax.all_to_all(x, 'tiles', split_axis=0, concat_axis=0, tiled=True)  30.6 us
    all_to_all x3, starting transfers between devices, exchange(): return lax.all_to_all(x, 'tiles', split_axis=0, concat_axis=0, tiled=True)  23.1 us
    pallas_call x1, Pallas kernels, shards(): call(adjoint_kernel, (sds((SLOTS, CHAN), bf16), sds((1, CHAN), f32)), 3,...  18.2 us
    all_to_all x3, waiting for transfers between devices, exchange(): return lax.all_to_all(x, 'tiles', split_axis=0, concat_axis=0, tiled=True)  13.3 us
    pallas_call x1, Pallas kernels, shards(): call(gather_feat, (sds((SLOTS, FEAT), bf16), sds((16, 128), jnp.int32)),...  5.6 us
    pallas_call x1, Pallas kernels, shards(): call(scatter_rows, sds((ROWS, FEAT), bf16), 2, scratch=[pltpu.VMEM((SLOTS...  4.21 us
  transfers between devices with their start and end apart: 3, of which 3 were waited for; matrix products, arithmetic and copies ran while one was open for 0% of the time, Pallas kernels for 28%

profile of v3, /device:TPU:1, one launch (start us, length us, event | category | flops | bytes accessed | tf_op | source)
XLA Modules:
  0.0 101.6 jit_solution(6208855434043940126)
XLA Ops:
  0.6 1.7 %gather_pos.1 = f32[128,128]{1,0:T(8,128)} custom-call(s32[16,128]{1,0:T(8,128)} %bitcast.23, s32[1,128]{1,0:T(1,128)} %count_hbm.1, f32[3,2048]{1,0:T(4,128)} %coords_hbm.1), custom_call_target="tpu_custom_call" | custom-call | tf_op jit(solution)/shard_map/gather_pos/pallas_call | solution.py:227
  2.4 11.5 %all-to-all-start = ((f32[128,1,128]{2,1,0:T(1,128)}), f32[128,1,128]{2,1,0:T(1,128)S(1)}, u32[]{:S(2)}, u32[]{:S(2)}) async-start(f32[128,1,128]{2,1,0:T(1,128)} %bitcast.22), calls=%async_computation | async-start | bytes 131072 | tf_op jit(solution)/shard_map/all_to_all | solution.py:221
  14.6 0.1 fusion.2
  14.6 0.1 fusion
  14.7 5.6 %gather_feat.1 = (bf16[2048,256]{1,0:T(8,128)(2,1)}, s32[16,128]{1,0:T(8,128)}) custom-call(s32[16,128]{1,0:T(8,128)} %bitcast.24, bf16[2048,256]{1,0:T(8,128)(2,1)} %feat_hbm.1), custom_call_target="tpu_custom_call" | custom-call | flops 4000000000 | bytes 2097152 | tf_op jit(solution)/shard_map/gather_feat/pallas_call | solution.py:238
  20.3 0.1 copy.11.trig_ref
  20.4 2.8 %all-to-all-done = f32[128,1,128]{2,1,0:T(1,128)S(1)} async-done(((f32[128,1,128]{2,1,0:T(1,128)}), f32[128,1,128]{2,1,0:T(1,128)S(1)}, u32[]{:S(2)}, u32[]{:S(2)}) %all-to-all-start) | async-done | bytes 65568 | tf_op jit(solution)/shard_map/all_to_all | solution.py:221
  23.2 6.9 %all-to-all-start.1 = ((bf16[128,16,256]{2,1,0:T(8,128)(2,1)}), bf16[128,16,256]{2,1,0:T(8,128)(2,1)S(1)}, u32[]{:S(2)}, u32[]{:S(2)}) async-start(bf16[128,16,256]{2,1,0:T(8,128)(2,1)} %bitcast.21), calls=%async_computation.1 | async-start | bytes 2097152 | tf_op jit(solution)/shard_map/all_to_all | solution.py:221
  30.2 0.0 copy-start
  30.2 18.2 %adjoint.1 = (bf16[2048,512]{1,0:T(8,128)(2,1)S(1)}, f32[1,512]{1,0:T(1,128)S(1)}) custom-call(f32[128,128]{1,0:T(8,128)S(1)} %bitcast.20, f32[64,4]{1,0:T(8,128)S(1)} %copy.11.trig_ref, bf16[4096,512]{1,0:T(8,128)(2,1)} %cot_hbm.1), custom_call_target="tpu_custom_call" | custom-call | flops 20000000000 | bytes 8388608 | tf_op jit(solution)/shard_map/adjoint/pallas_call | solution.py:251
  48.4 0.9 all-to-all-done.1
  49.3 0.0 copy-done
  49.3 1.5 %finish_tile.1 = bf16[32,4,5,8,128]{4,3,2,1,0:T(8,128)(2,1)S(1)} custom-call(bf16[2048,512]{1,0:T(8,128)(2,1)S(1)} %get-tuple-element.10.adj_ref, bf16[2048,256]{1,0:T(8,128)(2,1)S(1)} %bitcast.18, bf16[256,512]{1,0:T(8,128)(2,1)S(1)} %copy-done), custom_call_target="tpu_custom_call" | custom-call | tf_op jit(solution)/shard_map/finish_tile/pallas_call | solution.py:272
  50.8 30.6 %all_to_all.20.recv_ref = bf16[128,5,8,128]{3,2,1,0:T(8,128)(2,1)S(1)} all-to-all(bf16[128,5,8,128]{3,2,1,0:T(8,128)(2,1)S(1)} %bitcast.17), channel_id=1, replica_groups=mesh['tiles'=128] {'tiles'}, dimensions={0} | all-to-all | bytes 2621440 | tf_op jit(solution)/shard_map/all_to_all | solution.py:221
  81.4 0.0 copy-start.1
  81.4 1.0 reduce_block.1
  82.4 4.6 %all-to-all-start.3 = ((bf16[128,2,8,128]{3,2,1,0:T(8,128)(2,1)}), bf16[128,2,8,128]{3,2,1,0:T(8,128)(2,1)S(1)}, u32[]{:S(2)}, u32[]{:S(2)}) async-start(bf16[128,2,8,128]{3,2,1,0:T(8,128)(2,1)} %reduce_block.1), calls=%async_computation.3 | async-start | bytes 1048576 | tf_op jit(solution)/shard_map/all_to_all | solution.py:221
  87.0 0.0 copy-done.1
  87.0 4.2 %scatter_rows.1 = bf16[2048,256]{1,0:T(8,128)(2,1)} custom-call(s32[16,128]{1,0:T(8,128)S(1)} %copy-done.1, bf16[128,5,8,128]{3,2,1,0:T(8,128)(2,1)S(1)} %all_to_all.20.recv_ref), custom_call_target="tpu_custom_call" | custom-call | flops 4000000000 | bytes 3145728 | tf_op jit(solution)/shard_map/scatter_rows/pallas_call | solution.py:284
  91.2 9.5 %all-to-all-done.3 = bf16[128,2,8,128]{3,2,1,0:T(8,128)(2,1)S(1)} async-done(((bf16[128,2,8,128]{3,2,1,0:T(8,128)(2,1)}), bf16[128,2,8,128]{3,2,1,0:T(8,128)(2,1)S(1)}, u32[]{:S(2)}, u32[]{:S(2)}) %all-to-all-start.3) | async-done | bytes 524320 | tf_op jit(solution)/shard_map/all_to_all | solution.py:221
  100.7 0.9 assemble.1
  (1 shorter events, 0.0 us)
Async XLA Ops:
  2.4 20.8 %all-to-all-start = ((f32[128,1,128]{2,1,0:T(1,128)}), f32[128,1,128]{2,1,0:T(1,128)S(1)}, u32[]{:S(2)}, u32[]{:S(2)}) async-start(f32[128,1,128]{2,1,0:T(1,128)} %bitcast.22), calls=%async_computation | async-start | bytes 131072 | tf_op jit(solution)/shard_map/all_to_all | solution.py:221
  23.2 26.1 %all-to-all-start.1 = ((bf16[128,16,256]{2,1,0:T(8,128)(2,1)}), bf16[128,16,256]{2,1,0:T(8,128)(2,1)S(1)}, u32[]{:S(2)}, u32[]{:S(2)}) async-start(bf16[128,16,256]{2,1,0:T(8,128)(2,1)} %bitcast.21), calls=%async_computation.1 | async-start | bytes 2097152 | tf_op jit(solution)/shard_map/all_to_all | solution.py:221
  30.2 19.2 %copy-start = (bf16[256,512]{1,0:T(8,128)(2,1)S(1)}, bf16[256,512]{1,0:T(8,128)(2,1)}, u32[]{:S(2)}) copy-start(bf16[256,512]{1,0:T(8,128)(2,1)} %proj_hbm.1) | copy-start | bytes 786436
  81.4 5.6 %copy-start.1 = (s32[16,128]{1,0:T(8,128)S(1)}, s32[16,128]{1,0:T(8,128)}, u32[]{:S(2)}) copy-start(s32[16,128]{1,0:T(8,128)} %get-tuple-element.9.rl_ref) | copy-start | bytes 24580
  82.4 18.4 %all-to-all-start.3 = ((bf16[128,2,8,128]{3,2,1,0:T(8,128)(2,1)}), bf16[128,2,8,128]{3,2,1,0:T(8,128)(2,1)S(1)}, u32[]{:S(2)}, u32[]{:S(2)}) async-start(bf16[128,2,8,128]{3,2,1,0:T(8,128)(2,1)} %reduce_block.1), calls=%async_computation.3 | async-start | bytes 1048576 | tf_op jit(solution)/shard_map/all_to_all | solution.py:221

commit v4 on v3

--- a/solution.py
+++ b/solution.py
@@ -149,7 +149,7 @@
                 gacc_ref[:, cs] += jnp.sum((x * lg).reshape(16, 8, 128), axis=0)
         return 0
 
-    lax.fori_loop(0, 8, weigh, 0)
+    lax.fori_loop(0, 8, weigh, 0, unroll=2)
     gain_ref[...] = jnp.sum(gacc_ref[...], axis=0, keepdims=True) * (1.0 / 2048.0)
 
     def slots(n, _):
@@ -180,10 +180,9 @@
 
 def reduce_block(recv_ref, gain_ref, out_ref):
     total = jnp.sum(recv_ref[:, 4].astype(f32), axis=0)
-    g = jnp.concatenate([gain_ref[:, 128 * i : 128 * i + 128] for i in range(4)], axis=0)
-    hi = g.astype(bf16).astype(f32)
-    block = jnp.stack([total, jnp.concatenate([hi, g - hi], axis=0)]).astype(bf16)
-    out_ref[...] = jnp.broadcast_to(block[None], (N_DEV, 2, 8, 128))
+    g = [gain_ref[:, 128 * i : 128 * i + 128] for i in range(4)]
+    block = jnp.concatenate([total] + g, axis=0).reshape(3, 4, 128).astype(bf16)
+    out_ref[...] = jnp.broadcast_to(block[None], (N_DEV, 3, 4, 128))
 
 
 def scatter_rows(rl_ref, recv_ref, out_ref, val_ref, hot_ref):
@@ -203,11 +202,11 @@
 
 
 def assemble(x_ref, weight_ref, gain_ref):
-    total = jnp.zeros((8, 128), f32)
+    total = jnp.zeros((4, 128), f32)
     for cb in range(4):
-        weight_ref[:, 128 * cb : 128 * cb + 128] = x_ref[:, cb, 0].astype(f32).reshape(256, 128)
-        total = total + jnp.sum(x_ref[:, cb, 1].astype(f32), axis=0)
-    gain_ref[...] = total[0:4] + total[4:8]
+        weight_ref[:, 128 * cb : 128 * cb + 128] = x_ref[:, cb, 0:2].astype(f32).reshape(256, 128)
+        total = total + jnp.sum(x_ref[:, cb, 2].astype(f32), axis=0)
+    gain_ref[...] = total
 
 
 def trig_tables(tile):
@@ -233,6 +232,7 @@
         name="gather_pos",
         limit=60.47,
     )(rows, send_count, obs_coords)
+    msg, tile_id = lax.optimization_barrier((msg, tile_id))
     pos_in = exchange(msg.reshape(N_DEV, 1, 128)).reshape(N_DEV, 128)
 
     feat_out, rl = call(
@@ -279,7 +279,7 @@
         limit=24,
     )(adj, feat_in, projection)
     recv = exchange(out.reshape(N_DEV, 5, 8, 128))
-    block = call(reduce_block, sds((N_DEV, 2, 8, 128), bf16), 2, name="reduce_block", limit=8)(recv, gain)
+    block = call(reduce_block, sds((N_DEV, 3, 4, 128), bf16), 2, name="reduce_block", limit=8)(recv, gain)
     blocks = exchange(block)
     grad_obs = call(
         scatter_rows,
@@ -292,7 +292,7 @@
     )(rl, recv)
     weight, gain_sum = call(
         assemble, (sds((FEAT, CHAN), f32), sds((4, 128), f32)), 1, name="assemble", limit=8
-    )(blocks.reshape(32, 4, 2, 8, 128))
+    )(blocks.reshape(32, 4, 3, 4, 128))
     return grad_obs, weight, gain_sum.reshape(CHAN)
 
 

time: 102 us -> 100 us (0.980)
  waiting for transfers between devices: 13.3 us -> 12.1 us
    all_to_all x3, waiting for transfers between devices: 13.3 us -> 12.1 us  [exchange(): return lax.all_to_all(x, 'tiles', split_axis=0, concat_axis=0, tiled=True)]
where the time goes in v4:
time: 100 us
  Pallas kernels  32.8 us (33%)
  blocking collectives  30.3 us (30%)
  starting transfers between devices  23.1 us (23%)
  waiting for transfers between devices  12.1 us (12%)
  between operations  1.4 us (1%)
    all_to_all x1, blocking collectives, exchange(): return lax.all_to_all(x, 'tiles', split_axis=0, concat_axis=0, tiled=True)  30.3 us
    all_to_all x3, starting transfers between devices, exchange(): return lax.all_to_all(x, 'tiles', split_axis=0, concat_axis=0, tiled=True)  23.1 us
    pallas_call x1, Pallas kernels, shards(): call(adjoint_kernel, (sds((SLOTS, CHAN), bf16), sds((1, CHAN), f32)), 3,...  17.9 us
    all_to_all x3, waiting for transfers between devices, exchange(): return lax.all_to_all(x, 'tiles', split_axis=0, concat_axis=0, tiled=True)  12.1 us
    pallas_call x1, Pallas kernels, shards(): call(gather_feat, (sds((SLOTS, FEAT), bf16), sds((16, 128), jnp.int32)),...  5.6 us
    pallas_call x1, Pallas kernels, shards(): call(scatter_rows, sds((ROWS, FEAT), bf16), 2, scratch=[pltpu.VMEM((SLOTS...  4.2 us
  transfers between devices with their start and end apart: 3, of which 3 were waited for; matrix products, arithmetic and copies ran while one was open for 0% of the time, Pallas kernels for 28%

profile of v4, /device:TPU:1, one launch (start us, length us, event | category | flops | bytes accessed | tf_op | source)
XLA Modules:
  0.0 100.0 jit_solution(2163181407171814637)
XLA Ops:
  0.6 1.7 %gather_pos.1 = f32[128,128]{1,0:T(8,128)} custom-call(s32[16,128]{1,0:T(8,128)} %bitcast.23, s32[1,128]{1,0:T(1,128)} %count_hbm.1, f32[3,2048]{1,0:T(4,128)} %coords_hbm.1), custom_call_target="tpu_custom_call" | custom-call | tf_op jit(solution)/shard_map/gather_pos/pallas_call | solution.py:226
  2.4 11.5 %all-to-all-start = ((f32[128,1,128]{2,1,0:T(1,128)}), f32[128,1,128]{2,1,0:T(1,128)S(1)}, u32[]{:S(2)}, u32[]{:S(2)}) async-start(f32[128,1,128]{2,1,0:T(1,128)} %bitcast.22), calls=%async_computation | async-start | bytes 131072 | tf_op jit(solution)/shard_map/all_to_all | solution.py:220
  14.6 0.1 fusion.2
  14.6 0.1 fusion
  14.7 5.6 %gather_feat.1 = (bf16[2048,256]{1,0:T(8,128)(2,1)}, s32[16,128]{1,0:T(8,128)}) custom-call(s32[16,128]{1,0:T(8,128)} %bitcast.24, bf16[2048,256]{1,0:T(8,128)(2,1)} %feat_hbm.1), custom_call_target="tpu_custom_call" | custom-call | flops 4000000000 | bytes 2097152 | tf_op jit(solution)/shard_map/gather_feat/pallas_call | solution.py:238
  20.3 0.1 copy.11.trig_ref
  20.4 2.8 %all-to-all-done = f32[128,1,128]{2,1,0:T(1,128)S(1)} async-done(((f32[128,1,128]{2,1,0:T(1,128)}), f32[128,1,128]{2,1,0:T(1,128)S(1)}, u32[]{:S(2)}, u32[]{:S(2)}) %all-to-all-start) | async-done | bytes 65568 | tf_op jit(solution)/shard_map/all_to_all | solution.py:220
  23.2 6.9 %all-to-all-start.1 = ((bf16[128,16,256]{2,1,0:T(8,128)(2,1)}), bf16[128,16,256]{2,1,0:T(8,128)(2,1)S(1)}, u32[]{:S(2)}, u32[]{:S(2)}) async-start(bf16[128,16,256]{2,1,0:T(8,128)(2,1)} %bitcast.21), calls=%async_computation.1 | async-start | bytes 2097152 | tf_op jit(solution)/shard_map/all_to_all | solution.py:220
  30.2 0.0 copy-start
  30.2 17.9 %adjoint.1 = (bf16[2048,512]{1,0:T(8,128)(2,1)S(1)}, f32[1,512]{1,0:T(1,128)S(1)}) custom-call(f32[128,128]{1,0:T(8,128)S(1)} %bitcast.20, f32[64,4]{1,0:T(8,128)S(1)} %copy.11.trig_ref, bf16[4096,512]{1,0:T(8,128)(2,1)} %cot_hbm.1), custom_call_target="tpu_custom_call" | custom-call | flops 20000000000 | bytes 8388608 | tf_op jit(solution)/shard_map/adjoint/pallas_call | solution.py:251
  48.1 1.2 %all-to-all-done.1 = bf16[128,16,256]{2,1,0:T(8,128)(2,1)S(1)} async-done(((bf16[128,16,256]{2,1,0:T(8,128)(2,1)}), bf16[128,16,256]{2,1,0:T(8,128)(2,1)S(1)}, u32[]{:S(2)}, u32[]{:S(2)}) %all-to-all-start.1) | async-done | bytes 1048608 | tf_op jit(solution)/shard_map/all_to_all | solution.py:220
  49.3 0.0 copy-done
  49.3 1.5 %finish_tile.1 = bf16[32,4,5,8,128]{4,3,2,1,0:T(8,128)(2,1)S(1)} custom-call(bf16[2048,512]{1,0:T(8,128)(2,1)S(1)} %get-tuple-element.14.adj_ref, bf16[2048,256]{1,0:T(8,128)(2,1)S(1)} %bitcast.18, bf16[256,512]{1,0:T(8,128)(2,1)S(1)} %copy-done), custom_call_target="tpu_custom_call" | custom-call | tf_op jit(solution)/shard_map/finish_tile/pallas_call | solution.py:272
  50.8 0.0 copy-start.1
  50.9 30.3 %all_to_all.20.recv_ref = bf16[128,5,8,128]{3,2,1,0:T(8,128)(2,1)S(1)} all-to-all(bf16[128,5,8,128]{3,2,1,0:T(8,128)(2,1)S(1)} %bitcast.17), channel_id=1, replica_groups=mesh['tiles'=128] {'tiles'}, dimensions={0} | all-to-all | bytes 2621440 | tf_op jit(solution)/shard_map/all_to_all | solution.py:220
  81.1 0.9 reduce_block.1
  82.1 4.6 %all-to-all-start.3 = ((bf16[128,3,4,128]{3,2,1,0:T(4,128)(2,1)}), bf16[128,3,4,128]{3,2,1,0:T(4,128)(2,1)S(1)}, u32[]{:S(2)}, u32[]{:S(2)}) async-start(bf16[128,3,4,128]{3,2,1,0:T(4,128)(2,1)} %reduce_block.1), calls=%async_computation.3 | async-start | bytes 786432 | tf_op jit(solution)/shard_map/all_to_all | solution.py:220
  86.7 0.0 copy-done.1
  86.8 4.2 %scatter_rows.1 = bf16[2048,256]{1,0:T(8,128)(2,1)} custom-call(s32[16,128]{1,0:T(8,128)S(1)} %copy-done.1, bf16[128,5,8,128]{3,2,1,0:T(8,128)(2,1)S(1)} %all_to_all.20.recv_ref), custom_call_target="tpu_custom_call" | custom-call | flops 4000000000 | bytes 3145728 | tf_op jit(solution)/shard_map/scatter_rows/pallas_call | solution.py:284
  91.0 8.1 %all-to-all-done.3 = bf16[128,3,4,128]{3,2,1,0:T(4,128)(2,1)S(1)} async-done(((bf16[128,3,4,128]{3,2,1,0:T(4,128)(2,1)}), bf16[128,3,4,128]{3,2,1,0:T(4,128)(2,1)S(1)}, u32[]{:S(2)}, u32[]{:S(2)}) %all-to-all-start.3) | async-done | bytes 393248 | tf_op jit(solution)/shard_map/all_to_all | solution.py:220
  99.1 0.9 assemble.1
  (1 shorter events, 0.0 us)
Async XLA Ops:
  2.4 20.8 %all-to-all-start = ((f32[128,1,128]{2,1,0:T(1,128)}), f32[128,1,128]{2,1,0:T(1,128)S(1)}, u32[]{:S(2)}, u32[]{:S(2)}) async-start(f32[128,1,128]{2,1,0:T(1,128)} %bitcast.22), calls=%async_computation | async-start | bytes 131072 | tf_op jit(solution)/shard_map/all_to_all | solution.py:220
  23.2 26.1 %all-to-all-start.1 = ((bf16[128,16,256]{2,1,0:T(8,128)(2,1)}), bf16[128,16,256]{2,1,0:T(8,128)(2,1)S(1)}, u32[]{:S(2)}, u32[]{:S(2)}) async-start(bf16[128,16,256]{2,1,0:T(8,128)(2,1)} %bitcast.21), calls=%async_computation.1 | async-start | bytes 2097152 | tf_op jit(solution)/shard_map/all_to_all | solution.py:220
  30.2 19.2 %copy-start = (bf16[256,512]{1,0:T(8,128)(2,1)S(1)}, bf16[256,512]{1,0:T(8,128)(2,1)}, u32[]{:S(2)}) copy-start(bf16[256,512]{1,0:T(8,128)(2,1)} %proj_hbm.1) | copy-start | bytes 786436
  50.8 35.9 %copy-start.1 = (s32[16,128]{1,0:T(8,128)S(1)}, s32[16,128]{1,0:T(8,128)}, u32[]{:S(2)}) copy-start(s32[16,128]{1,0:T(8,128)} %get-tuple-element.11.rl_ref) | copy-start | bytes 24580
  82.1 17.0 %all-to-all-start.3 = ((bf16[128,3,4,128]{3,2,1,0:T(4,128)(2,1)}), bf16[128,3,4,128]{3,2,1,0:T(4,128)(2,1)S(1)}, u32[]{:S(2)}, u32[]{:S(2)}) async-start(bf16[128,3,4,128]{3,2,1,0:T(4,128)(2,1)} %reduce_block.1), calls=%async_computation.3 | async-start | bytes 786432 | tf_op jit(solution)/shard_map/all_to_all | solution.py:220

commit v5 on v4

--- a/solution.py
+++ b/solution.py
@@ -93,10 +93,15 @@
 
 
 def adjoint_kernel(
-    recv_ref, trig_ref, cot_hbm, adj_ref, gain_ref, c_ref, v_ref, m_ref, k_ref, w_ref, dens_ref, cot_ref, gacc_ref, sem
+    recv_ref, trig_ref, cot_hbm, adj_ref, gain_ref, c_ref, v_ref, m_ref, k_ref, w_ref, cot_ref, gacc_ref, sem
 ):
-    load = pltpu.make_async_copy(cot_hbm, cot_ref, sem)
-    load.start()
+    def load(g):
+        part = pl.ds(pl.multiple_of(g * 512, 512), 512)
+        return pltpu.make_async_copy(cot_hbm.at[part], cot_ref.at[part], sem.at[g])
+
+    for g in range(8):
+        load(g).start()
+    gacc_ref[...] = jnp.zeros_like(gacc_ref)
     cl, sl, cp, sp = [jnp.broadcast_to(trig_ref[:, i : i + 1], (64, 128)) for i in range(4)]
     c_ref[...] = cp
     x, y, z = [slot_major(recv_ref[:, 16 * c : 16 * c + 16]) for c in range(3)]
@@ -109,11 +114,25 @@
         v_ref[:, cs] = (-KAPPA * rho) * ((cl - px * inv) ** 2 + (sl - py * inv) ** 2)
         m_ref[:, cs] = -KAPPA * ((cp - rho) ** 2 + (sp - pz) ** 2)
 
-    def group(g, _):
+    def columns(dens):
+        sc = jnp.broadcast_to(1.0 / (1.0 + dens), (128, 128)).T
+        lg = jnp.broadcast_to(jnp.log1p(dens), (128, 128)).T
+        return sc, lg
+
+    def weigh(row, q, sc, lg):
+        rs = pl.ds(pl.multiple_of(row, 128), 128)
+        cs = slice(128 * q, 128 * q + 128)
+        x = cot_ref[rs, cs].astype(f32)
+        w_ref[rs, cs] = (x * sc).astype(bf16)
+        gacc_ref[:, cs] += jnp.sum((x * lg).reshape(16, 8, 128), axis=0)
+
+    def group(g, dens):
         base = pl.multiple_of(g * 8, 8)
+        before = jnp.maximum(g - 1, 0) * 512
         cc = c_ref[pl.ds(base, 8), :]
         rows = []
         for m in range(4):
+            sc, lg = columns(dens[m : m + 1, :])
             ds = []
             for h in range(2):
                 i = 2 * m + h
@@ -126,30 +145,22 @@
                     d = d + k
                     k_ref[pl.ds(pl.multiple_of(g * 512, 512) + 64 * i, 64), cs] = k.astype(bf16)
                 ds.append(d)
+                weigh(before + 128 * m, 2 * h, sc, lg)
+                weigh(before + 128 * m, 2 * h + 1, sc, lg)
             rows.append(jnp.sum(jnp.concatenate(ds, axis=0).T, axis=0, keepdims=True))
-        dens_ref[g] = jnp.concatenate(rows, axis=0)
-        return 0
-
-    lax.fori_loop(0, 8, group, 0)
-    load.wait()
-    gacc_ref[...] = jnp.zeros_like(gacc_ref)
-
-    def weigh(g, _):
-        dens = dens_ref[g]
-        scale = 1.0 / (1.0 + dens)
-        logd = jnp.log1p(dens)
-        for m in range(4):
-            rs = pl.ds(pl.multiple_of(g * 512 + 128 * m, 128), 128)
-            sc = jnp.broadcast_to(scale[m : m + 1, :], (128, 128)).T
-            lg = jnp.broadcast_to(logd[m : m + 1, :], (128, 128)).T
-            for q in range(4):
-                cs = slice(128 * q, 128 * q + 128)
-                x = cot_ref[rs, cs].astype(f32)
-                w_ref[rs, cs] = (x * sc).astype(bf16)
-                gacc_ref[:, cs] += jnp.sum((x * lg).reshape(16, 8, 128), axis=0)
-        return 0
-
-    lax.fori_loop(0, 8, weigh, 0, unroll=2)
+
+        @pl.when(g < 7)
+        def _():
+            load(g + 1).wait()
+
+        return jnp.concatenate(rows, axis=0)
+
+    load(0).wait()
+    dens = lax.fori_loop(0, 8, group, jnp.zeros((4, 128), f32))
+    for m in range(4):
+        sc, lg = columns(dens[m : m + 1, :])
+        for q in range(4):
+            weigh(7 * 512 + 128 * m, q, sc, lg)
     gain_ref[...] = jnp.sum(gacc_ref[...], axis=0, keepdims=True) * (1.0 / 2048.0)
 
     def slots(n, _):
@@ -259,10 +270,9 @@
             pltpu.VMEM((64, SLOTS), f32),
             pltpu.VMEM((CELLS, SLOTS), bf16),
             pltpu.VMEM((CELLS, CHAN), bf16),
-            pltpu.VMEM((8, 4, 128), f32),
             pltpu.VMEM((CELLS, CHAN), bf16),
             pltpu.VMEM((8, CHAN), f32),
-            DMA,
+            DMA((8,)),
         ],
         name="adjoint",
         limit=48,

time: 100 us -> 100 us (level)
  no operation moved by 1% of the time
where the time goes in v5:
time: 100 us; the launch traced here: 99.9 us
  Pallas kernels  32.7 us (33%)
  blocking collectives  30.2 us (30%)
  starting transfers between devices  23.1 us (23%)
  waiting for transfers between devices  12.2 us (12%)
  between operations  1.4 us (1%)
    all_to_all x1, blocking collectives, exchange(): return lax.all_to_all(x, 'tiles', split_axis=0, concat_axis=0, tiled=True)  30.2 us
    all_to_all x3, starting transfers between devices, exchange(): return lax.all_to_all(x, 'tiles', split_axis=0, concat_axis=0, tiled=True)  23.1 us
    pallas_call x1, Pallas kernels, shards(): call(adjoint_kernel, (sds((SLOTS, CHAN), bf16), sds((1, CHAN), f32)), 3,...  17.9 us
    all_to_all x3, waiting for transfers between devices, exchange(): return lax.all_to_all(x, 'tiles', split_axis=0, concat_axis=0, tiled=True)  12.2 us
    pallas_call x1, Pallas kernels, shards(): call(gather_feat, (sds((SLOTS, FEAT), bf16), sds((16, 128), jnp.int32)),...  5.6 us
    pallas_call x1, Pallas kernels, shards(): call(scatter_rows, sds((ROWS, FEAT), bf16), 2, scratch=[pltpu.VMEM((SLOTS...  4.2 us
  transfers between devices with their start and end apart: 3, of which 3 were waited for; matrix products, arithmetic and copies ran while one was open for 0% of the time, Pallas kernels for 28%

profile of v5, /device:TPU:1, one launch (start us, length us, event | category | flops | bytes accessed | tf_op | source)
XLA Modules:
  0.0 99.9 jit_solution(15740186388641873247)
XLA Ops:
  0.6 1.7 %gather_pos.1 = f32[128,128]{1,0:T(8,128)} custom-call(s32[16,128]{1,0:T(8,128)} %bitcast.23, s32[1,128]{1,0:T(1,128)} %count_hbm.1, f32[3,2048]{1,0:T(4,128)} %coords_hbm.1), custom_call_target="tpu_custom_call" | custom-call | tf_op jit(solution)/shard_map/gather_pos/pallas_call | solution.py:237
  2.4 11.5 %all-to-all-start = ((f32[128,1,128]{2,1,0:T(1,128)}), f32[128,1,128]{2,1,0:T(1,128)S(1)}, u32[]{:S(2)}, u32[]{:S(2)}) async-start(f32[128,1,128]{2,1,0:T(1,128)} %bitcast.22), calls=%async_computation | async-start | bytes 131072 | tf_op jit(solution)/shard_map/all_to_all | solution.py:231
  14.6 0.1 fusion.2
  14.6 0.1 fusion
  14.7 5.6 %gather_feat.1 = (bf16[2048,256]{1,0:T(8,128)(2,1)}, s32[16,128]{1,0:T(8,128)}) custom-call(s32[16,128]{1,0:T(8,128)} %bitcast.24, bf16[2048,256]{1,0:T(8,128)(2,1)} %feat_hbm.1), custom_call_target="tpu_custom_call" | custom-call | flops 4000000000 | bytes 2097152 | tf_op jit(solution)/shard_map/gather_feat/pallas_call | solution.py:249
  20.3 0.1 copy.11.trig_ref
  20.4 2.8 %all-to-all-done = f32[128,1,128]{2,1,0:T(1,128)S(1)} async-done(((f32[128,1,128]{2,1,0:T(1,128)}), f32[128,1,128]{2,1,0:T(1,128)S(1)}, u32[]{:S(2)}, u32[]{:S(2)}) %all-to-all-start) | async-done | bytes 65568 | tf_op jit(solution)/shard_map/all_to_all | solution.py:231
  23.2 6.9 %all-to-all-start.1 = ((bf16[128,16,256]{2,1,0:T(8,128)(2,1)}), bf16[128,16,256]{2,1,0:T(8,128)(2,1)S(1)}, u32[]{:S(2)}, u32[]{:S(2)}) async-start(bf16[128,16,256]{2,1,0:T(8,128)(2,1)} %bitcast.21), calls=%async_computation.1 | async-start | bytes 2097152 | tf_op jit(solution)/shard_map/all_to_all | solution.py:231
  30.2 0.0 copy-start
  30.2 17.9 %adjoint.1 = (bf16[2048,512]{1,0:T(8,128)(2,1)S(1)}, f32[1,512]{1,0:T(1,128)S(1)}) custom-call(f32[128,128]{1,0:T(8,128)S(1)} %bitcast.20, f32[64,4]{1,0:T(8,128)S(1)} %copy.11.trig_ref, bf16[4096,512]{1,0:T(8,128)(2,1)} %cot_hbm.1), custom_call_target="tpu_custom_call" | custom-call | flops 20000000000 | bytes 8388608 | tf_op jit(solution)/shard_map/adjoint/pallas_call | solution.py:262
  48.0 1.3 %all-to-all-done.1 = bf16[128,16,256]{2,1,0:T(8,128)(2,1)S(1)} async-done(((bf16[128,16,256]{2,1,0:T(8,128)(2,1)}), bf16[128,16,256]{2,1,0:T(8,128)(2,1)S(1)}, u32[]{:S(2)}, u32[]{:S(2)}) %all-to-all-start.1) | async-done | bytes 1048608 | tf_op jit(solution)/shard_map/all_to_all | solution.py:231
  49.3 0.0 copy-done
  49.3 1.5 %finish_tile.1 = bf16[32,4,5,8,128]{4,3,2,1,0:T(8,128)(2,1)S(1)} custom-call(bf16[2048,512]{1,0:T(8,128)(2,1)S(1)} %get-tuple-element.14.adj_ref, bf16[2048,256]{1,0:T(8,128)(2,1)S(1)} %bitcast.18, bf16[256,512]{1,0:T(8,128)(2,1)S(1)} %copy-done), custom_call_target="tpu_custom_call" | custom-call | tf_op jit(solution)/shard_map/finish_tile/pallas_call | solution.py:282
  50.8 0.0 copy-start.1
  50.9 30.2 %all_to_all.20.recv_ref = bf16[128,5,8,128]{3,2,1,0:T(8,128)(2,1)S(1)} all-to-all(bf16[128,5,8,128]{3,2,1,0:T(8,128)(2,1)S(1)} %bitcast.17), channel_id=1, replica_groups=mesh['tiles'=128] {'tiles'}, dimensions={0} | all-to-all | bytes 2621440 | tf_op jit(solution)/shard_map/all_to_all | solution.py:231
  81.1 0.9 reduce_block.1
  82.0 4.6 %all-to-all-start.3 = ((bf16[128,3,4,128]{3,2,1,0:T(4,128)(2,1)}), bf16[128,3,4,128]{3,2,1,0:T(4,128)(2,1)S(1)}, u32[]{:S(2)}, u32[]{:S(2)}) async-start(bf16[128,3,4,128]{3,2,1,0:T(4,128)(2,1)} %reduce_block.1), calls=%async_computation.3 | async-start | bytes 786432 | tf_op jit(solution)/shard_map/all_to_all | solution.py:231
  86.7 0.0 copy-done.1
  86.7 4.2 %scatter_rows.1 = bf16[2048,256]{1,0:T(8,128)(2,1)} custom-call(s32[16,128]{1,0:T(8,128)S(1)} %copy-done.1, bf16[128,5,8,128]{3,2,1,0:T(8,128)(2,1)S(1)} %all_to_all.20.recv_ref), custom_call_target="tpu_custom_call" | custom-call | flops 4000000000 | bytes 3145728 | tf_op jit(solution)/shard_map/scatter_rows/pallas_call | solution.py:294
  90.9 8.1 %all-to-all-done.3 = bf16[128,3,4,128]{3,2,1,0:T(4,128)(2,1)S(1)} async-done(((bf16[128,3,4,128]{3,2,1,0:T(4,128)(2,1)}), bf16[128,3,4,128]{3,2,1,0:T(4,128)(2,1)S(1)}, u32[]{:S(2)}, u32[]{:S(2)}) %all-to-all-start.3) | async-done | bytes 393248 | tf_op jit(solution)/shard_map/all_to_all | solution.py:231
  99.0 0.9 assemble.1
  (1 shorter events, 0.0 us)
Async XLA Ops:
  2.4 20.8 %all-to-all-start = ((f32[128,1,128]{2,1,0:T(1,128)}), f32[128,1,128]{2,1,0:T(1,128)S(1)}, u32[]{:S(2)}, u32[]{:S(2)}) async-start(f32[128,1,128]{2,1,0:T(1,128)} %bitcast.22), calls=%async_computation | async-start | bytes 131072 | tf_op jit(solution)/shard_map/all_to_all | solution.py:231
  23.2 26.1 %all-to-all-start.1 = ((bf16[128,16,256]{2,1,0:T(8,128)(2,1)}), bf16[128,16,256]{2,1,0:T(8,128)(2,1)S(1)}, u32[]{:S(2)}, u32[]{:S(2)}) async-start(bf16[128,16,256]{2,1,0:T(8,128)(2,1)} %bitcast.21), calls=%async_computation.1 | async-start | bytes 2097152 | tf_op jit(solution)/shard_map/all_to_all | solution.py:231
  30.2 19.2 %copy-start = (bf16[256,512]{1,0:T(8,128)(2,1)S(1)}, bf16[256,512]{1,0:T(8,128)(2,1)}, u32[]{:S(2)}) copy-start(bf16[256,512]{1,0:T(8,128)(2,1)} %proj_hbm.1) | copy-start | bytes 786436
  50.8 35.8 %copy-start.1 = (s32[16,128]{1,0:T(8,128)S(1)}, s32[16,128]{1,0:T(8,128)}, u32[]{:S(2)}) copy-start(s32[16,128]{1,0:T(8,128)} %get-tuple-element.11.rl_ref) | copy-start | bytes 24580
  82.0 17.0 %all-to-all-start.3 = ((bf16[128,3,4,128]{3,2,1,0:T(4,128)(2,1)}), bf16[128,3,4,128]{3,2,1,0:T(4,128)(2,1)S(1)}, u32[]{:S(2)}, u32[]{:S(2)}) async-start(bf16[128,3,4,128]{3,2,1,0:T(4,128)(2,1)} %reduce_block.1), calls=%async_computation.3 | async-start | bytes 786432 | tf_op jit(solution)/shard_map/all_to_all | solution.py:231

commit v6 on v5

--- a/solution.py
+++ b/solution.py
@@ -128,11 +128,12 @@
 
     def group(g, dens):
         base = pl.multiple_of(g * 8, 8)
-        before = jnp.maximum(g - 1, 0) * 512
+        before = (g - 1) * 512
         cc = c_ref[pl.ds(base, 8), :]
         rows = []
         for m in range(4):
-            sc, lg = columns(dens[m : m + 1, :])
+            if dens is not None:
+                sc, lg = columns(dens[m : m + 1, :])
             ds = []
             for h in range(2):
                 i = 2 * m + h
@@ -145,18 +146,14 @@
                     d = d + k
                     k_ref[pl.ds(pl.multiple_of(g * 512, 512) + 64 * i, 64), cs] = k.astype(bf16)
                 ds.append(d)
-                weigh(before + 128 * m, 2 * h, sc, lg)
-                weigh(before + 128 * m, 2 * h + 1, sc, lg)
+                if dens is not None:
+                    weigh(before + 128 * m, 2 * h, sc, lg)
+                    weigh(before + 128 * m, 2 * h + 1, sc, lg)
             rows.append(jnp.sum(jnp.concatenate(ds, axis=0).T, axis=0, keepdims=True))
-
-        @pl.when(g < 7)
-        def _():
-            load(g + 1).wait()
-
+        load(g).wait()
         return jnp.concatenate(rows, axis=0)
 
-    load(0).wait()
-    dens = lax.fori_loop(0, 8, group, jnp.zeros((4, 128), f32))
+    dens = lax.fori_loop(1, 8, group, group(0, None))
     for m in range(4):
         sc, lg = columns(dens[m : m + 1, :])
         for q in range(4):

time: 100 us -> 99.6 us (level)
  transfers between devices with their start and end apart: 3 -> 3, of which waited for: 3 -> 3; matrix products, arithmetic and copies ran while one was open for 0% -> 0% of each run, Pallas kernels for 28% -> 27%
where the time goes in v6:
time: 99.6 us; the launch traced here: 99.2 us
  Pallas kernels  32.1 us (32%)
  blocking collectives  29.6 us (30%)
  starting transfers between devices  23.1 us (23%)
  waiting for transfers between devices  12.9 us (13%)
  between operations  1.4 us (1%)
    all_to_all x1, blocking collectives, exchange(): return lax.all_to_all(x, 'tiles', split_axis=0, concat_axis=0, tiled=True)  29.6 us
    all_to_all x3, starting transfers between devices, exchange(): return lax.all_to_all(x, 'tiles', split_axis=0, concat_axis=0, tiled=True)  23.1 us
    pallas_call x1, Pallas kernels, shards(): call(adjoint_kernel, (sds((SLOTS, CHAN), bf16), sds((1, CHAN), f32)), 3,...  17.2 us
    all_to_all x3, waiting for transfers between devices, exchange(): return lax.all_to_all(x, 'tiles', split_axis=0, concat_axis=0, tiled=True)  12.9 us
    pallas_call x1, Pallas kernels, shards(): call(gather_feat, (sds((SLOTS, FEAT), bf16), sds((16, 128), jnp.int32)),...  5.6 us
    pallas_call x1, Pallas kernels, shards(): call(scatter_rows, sds((ROWS, FEAT), bf16), 2, scratch=[pltpu.VMEM((SLOTS...  4.21 us
  transfers between devices with their start and end apart: 3, of which 3 were waited for; matrix products, arithmetic and copies ran while one was open for 0% of the time, Pallas kernels for 27%

profile of v6, /device:TPU:1, one launch (start us, length us, event | category | flops | bytes accessed | tf_op | source)
XLA Modules:
  0.0 99.2 jit_solution(18432942314088069191)
XLA Ops:
  0.6 1.7 %gather_pos.1 = f32[128,128]{1,0:T(8,128)} custom-call(s32[16,128]{1,0:T(8,128)} %bitcast.23, s32[1,128]{1,0:T(1,128)} %count_hbm.1, f32[3,2048]{1,0:T(4,128)} %coords_hbm.1), custom_call_target="tpu_custom_call" | custom-call | tf_op jit(solution)/shard_map/gather_pos/pallas_call | solution.py:234
  2.4 11.5 %all-to-all-start = ((f32[128,1,128]{2,1,0:T(1,128)}), f32[128,1,128]{2,1,0:T(1,128)S(1)}, u32[]{:S(2)}, u32[]{:S(2)}) async-start(f32[128,1,128]{2,1,0:T(1,128)} %bitcast.22), calls=%async_computation | async-start | bytes 131072 | tf_op jit(solution)/shard_map/all_to_all | solution.py:228
  14.6 0.1 fusion.2
  14.6 0.1 fusion
  14.7 5.6 %gather_feat.1 = (bf16[2048,256]{1,0:T(8,128)(2,1)}, s32[16,128]{1,0:T(8,128)}) custom-call(s32[16,128]{1,0:T(8,128)} %bitcast.24, bf16[2048,256]{1,0:T(8,128)(2,1)} %feat_hbm.1), custom_call_target="tpu_custom_call" | custom-call | flops 4000000000 | bytes 2097152 | tf_op jit(solution)/shard_map/gather_feat/pallas_call | solution.py:246
  20.3 0.1 copy.11.trig_ref
  20.4 2.8 %all-to-all-done = f32[128,1,128]{2,1,0:T(1,128)S(1)} async-done(((f32[128,1,128]{2,1,0:T(1,128)}), f32[128,1,128]{2,1,0:T(1,128)S(1)}, u32[]{:S(2)}, u32[]{:S(2)}) %all-to-all-start) | async-done | bytes 65568 | tf_op jit(solution)/shard_map/all_to_all | solution.py:228
  23.2 6.9 %all-to-all-start.1 = ((bf16[128,16,256]{2,1,0:T(8,128)(2,1)}), bf16[128,16,256]{2,1,0:T(8,128)(2,1)S(1)}, u32[]{:S(2)}, u32[]{:S(2)}) async-start(bf16[128,16,256]{2,1,0:T(8,128)(2,1)} %bitcast.21), calls=%async_computation.1 | async-start | bytes 2097152 | tf_op jit(solution)/shard_map/all_to_all | solution.py:228
  30.2 0.0 copy-start
  30.2 17.2 %adjoint.1 = (bf16[2048,512]{1,0:T(8,128)(2,1)S(1)}, f32[1,512]{1,0:T(1,128)S(1)}) custom-call(f32[128,128]{1,0:T(8,128)S(1)} %bitcast.20, f32[64,4]{1,0:T(8,128)S(1)} %copy.11.trig_ref, bf16[4096,512]{1,0:T(8,128)(2,1)} %cot_hbm.1), custom_call_target="tpu_custom_call" | custom-call | flops 20000000000 | bytes 8388608 | tf_op jit(solution)/shard_map/adjoint/pallas_call | solution.py:259
  47.4 1.9 %all-to-all-done.1 = bf16[128,16,256]{2,1,0:T(8,128)(2,1)S(1)} async-done(((bf16[128,16,256]{2,1,0:T(8,128)(2,1)}), bf16[128,16,256]{2,1,0:T(8,128)(2,1)S(1)}, u32[]{:S(2)}, u32[]{:S(2)}) %all-to-all-start.1) | async-done | bytes 1048608 | tf_op jit(solution)/shard_map/all_to_all | solution.py:228
  49.3 0.0 copy-done
  49.3 1.5 %finish_tile.1 = bf16[32,4,5,8,128]{4,3,2,1,0:T(8,128)(2,1)S(1)} custom-call(bf16[2048,512]{1,0:T(8,128)(2,1)S(1)} %get-tuple-element.14.adj_ref, bf16[2048,256]{1,0:T(8,128)(2,1)S(1)} %bitcast.18, bf16[256,512]{1,0:T(8,128)(2,1)S(1)} %copy-done), custom_call_target="tpu_custom_call" | custom-call | tf_op jit(solution)/shard_map/finish_tile/pallas_call | solution.py:279
  50.8 0.0 copy-start.1
  50.8 29.6 %all_to_all.20.recv_ref = bf16[128,5,8,128]{3,2,1,0:T(8,128)(2,1)S(1)} all-to-all(bf16[128,5,8,128]{3,2,1,0:T(8,128)(2,1)S(1)} %bitcast.17), channel_id=1, replica_groups=mesh['tiles'=128] {'tiles'}, dimensions={0} | all-to-all | bytes 2621440 | tf_op jit(solution)/shard_map/all_to_all | solution.py:228
  80.4 0.9 reduce_block.1
  81.3 4.6 %all-to-all-start.3 = ((bf16[128,3,4,128]{3,2,1,0:T(4,128)(2,1)}), bf16[128,3,4,128]{3,2,1,0:T(4,128)(2,1)S(1)}, u32[]{:S(2)}, u32[]{:S(2)}) async-start(bf16[128,3,4,128]{3,2,1,0:T(4,128)(2,1)} %reduce_block.1), calls=%async_computation.3 | async-start | bytes 786432 | tf_op jit(solution)/shard_map/all_to_all | solution.py:228
  86.0 0.0 copy-done.1
  86.0 4.2 %scatter_rows.1 = bf16[2048,256]{1,0:T(8,128)(2,1)} custom-call(s32[16,128]{1,0:T(8,128)S(1)} %copy-done.1, bf16[128,5,8,128]{3,2,1,0:T(8,128)(2,1)S(1)} %all_to_all.20.recv_ref), custom_call_target="tpu_custom_call" | custom-call | flops 4000000000 | bytes 3145728 | tf_op jit(solution)/shard_map/scatter_rows/pallas_call | solution.py:291
  90.2 8.1 %all-to-all-done.3 = bf16[128,3,4,128]{3,2,1,0:T(4,128)(2,1)S(1)} async-done(((bf16[128,3,4,128]{3,2,1,0:T(4,128)(2,1)}), bf16[128,3,4,128]{3,2,1,0:T(4,128)(2,1)S(1)}, u32[]{:S(2)}, u32[]{:S(2)}) %all-to-all-start.3) | async-done | bytes 393248 | tf_op jit(solution)/shard_map/all_to_all | solution.py:228
  98.3 0.9 assemble.1
  (1 shorter events, 0.0 us)
Async XLA Ops:
  2.4 20.8 %all-to-all-start = ((f32[128,1,128]{2,1,0:T(1,128)}), f32[128,1,128]{2,1,0:T(1,128)S(1)}, u32[]{:S(2)}, u32[]{:S(2)}) async-start(f32[128,1,128]{2,1,0:T(1,128)} %bitcast.22), calls=%async_computation | async-start | bytes 131072 | tf_op jit(solution)/shard_map/all_to_all | solution.py:228
  23.2 26.1 %all-to-all-start.1 = ((bf16[128,16,256]{2,1,0:T(8,128)(2,1)}), bf16[128,16,256]{2,1,0:T(8,128)(2,1)S(1)}, u32[]{:S(2)}, u32[]{:S(2)}) async-start(bf16[128,16,256]{2,1,0:T(8,128)(2,1)} %bitcast.21), calls=%async_computation.1 | async-start | bytes 2097152 | tf_op jit(solution)/shard_map/all_to_all | solution.py:228
  30.2 19.2 %copy-start = (bf16[256,512]{1,0:T(8,128)(2,1)S(1)}, bf16[256,512]{1,0:T(8,128)(2,1)}, u32[]{:S(2)}) copy-start(bf16[256,512]{1,0:T(8,128)(2,1)} %proj_hbm.1) | copy-start | bytes 786436
  50.8 35.2 %copy-start.1 = (s32[16,128]{1,0:T(8,128)S(1)}, s32[16,128]{1,0:T(8,128)}, u32[]{:S(2)}) copy-start(s32[16,128]{1,0:T(8,128)} %get-tuple-element.11.rl_ref) | copy-start | bytes 24580
  81.3 17.0 %all-to-all-start.3 = ((bf16[128,3,4,128]{3,2,1,0:T(4,128)(2,1)}), bf16[128,3,4,128]{3,2,1,0:T(4,128)(2,1)S(1)}, u32[]{:S(2)}, u32[]{:S(2)}) async-start(bf16[128,3,4,128]{3,2,1,0:T(4,128)(2,1)} %reduce_block.1), calls=%async_computation.3 | async-start | bytes 786432 | tf_op jit(solution)/shard_map/all_to_all | solution.py:228

commit v7 on v6

--- a/solution.py
+++ b/solution.py
@@ -93,7 +93,8 @@
 
 
 def adjoint_kernel(
-    recv_ref, trig_ref, cot_hbm, adj_ref, gain_ref, c_ref, v_ref, m_ref, k_ref, w_ref, cot_ref, gacc_ref, sem
+    recv_ref, trig_ref, cot_hbm, proj_hbm, adj_ref, slot_ref, gain_ref,
+    c_ref, v_ref, m_ref, k_ref, w_ref, cot_ref, gacc_ref, proj_ref, sem,
 ):
     def load(g):
         part = pl.ds(pl.multiple_of(g * 512, 512), 512)
@@ -101,6 +102,8 @@
 
     for g in range(8):
         load(g).start()
+    load_proj = pltpu.make_async_copy(proj_hbm, proj_ref, sem.at[8])
+    load_proj.start()
     gacc_ref[...] = jnp.zeros_like(gacc_ref)
     cl, sl, cp, sp = [jnp.broadcast_to(trig_ref[:, i : i + 1], (64, 128)) for i in range(4)]
     c_ref[...] = cp
@@ -160,30 +163,29 @@
             weigh(7 * 512 + 128 * m, q, sc, lg)
     gain_ref[...] = jnp.sum(gacc_ref[...], axis=0, keepdims=True) * (1.0 / 2048.0)
 
+    load_proj.wait()
+
     def slots(n, _):
         rs = pl.ds(pl.multiple_of(n * 1024, 1024), 1024)
-        adj_ref[rs, :] = lax.dot_general(
+        a = lax.dot_general(
             k_ref[:, rs], w_ref[...], (((0,), (0,)), ((), ())), preferred_element_type=f32
         ).astype(bf16)
+        adj_ref[rs, :] = a
+        s = lax.dot_general(a, proj_ref[...], (((1,), (1,)), ((), ())), preferred_element_type=f32).astype(bf16)
+        for h in range(2):
+            part = s[:, 128 * h : 128 * h + 128].reshape(16, 4, 2, 8, 128)
+            slot_ref[pl.ds(pl.multiple_of(n * 16, 16), 16), :, 2 * h : 2 * h + 2] = part
         return 0
 
     lax.fori_loop(0, SLOTS // 1024, slots, 0)
 
 
-def finish_tile(adj_ref, feat_ref, proj_hbm, out_ref, proj_ref, sems):
-    load = load_all([(proj_hbm, proj_ref)], sems)[0]
+def finish_tile(adj_ref, slot_ref, feat_ref, out_ref):
     w = lax.dot_general(feat_ref[...], adj_ref[...], (((0,), (0,)), ((), ())), preferred_element_type=f32)
+    out_ref[:, :, 0:4] = slot_ref[...]
     w = (w * (1.0 / 256.0)).astype(bf16)
     for cb in range(4):
         out_ref[:, cb, 4] = w[:, 128 * cb : 128 * cb + 128].reshape(32, 8, 128)
-    load.wait()
-    for n in range(SLOTS // 512):
-        s = lax.dot_general(
-            adj_ref[512 * n : 512 * n + 512, :], proj_ref[...], (((1,), (1,)), ((), ())), preferred_element_type=f32
-        ).astype(bf16)
-        for h in range(2):
-            t = s[:, 128 * h : 128 * h + 128]
-            out_ref[8 * n : 8 * n + 8, :, 2 * h : 2 * h + 2] = t.reshape(8, 4, 2, 8, 128)
 
 
 def reduce_block(recv_ref, gain_ref, out_ref):
@@ -256,11 +258,11 @@
     trig = trig_tables(tile_id[0])
 
     feat_in = exchange(feat_out.reshape(N_DEV, CAP, FEAT)).reshape(SLOTS, FEAT)
-    adj, gain = call(
+    adj, slot, gain = call(
         adjoint_kernel,
-        (sds((SLOTS, CHAN), bf16), sds((1, CHAN), f32)),
-        3,
-        in_specs=[VM, VM, HBM],
+        (sds((SLOTS, CHAN), bf16), sds((32, 4, 4, 8, 128), bf16), sds((1, CHAN), f32)),
+        4,
+        in_specs=[VM, VM, HBM, HBM],
         scratch=[
             pltpu.VMEM((64, 128), f32),
             pltpu.VMEM((64, SLOTS), f32),
@@ -269,22 +271,21 @@
             pltpu.VMEM((CELLS, CHAN), bf16),
             pltpu.VMEM((CELLS, CHAN), bf16),
             pltpu.VMEM((8, CHAN), f32),
-            DMA((8,)),
+            pltpu.VMEM((FEAT, CHAN), bf16),
+            DMA((9,)),
         ],
         name="adjoint",
         limit=48,
         cost=cost(20 * 10**9, 8 * 2**20),
-    )(pos_in, trig, cotangent)
+    )(pos_in, trig, cotangent, projection)
 
     out = call(
         finish_tile,
         sds((32, 4, 5, 8, 128), bf16),
         3,
-        in_specs=[VM, VM, HBM],
-        scratch=[pltpu.VMEM((FEAT, CHAN), bf16), DMA((1,))],
         name="finish_tile",
         limit=24,
-    )(adj, feat_in, projection)
+    )(adj, slot, feat_in)
     recv = exchange(out.reshape(N_DEV, 5, 8, 128))
     block = call(reduce_block, sds((N_DEV, 3, 4, 128), bf16), 2, name="reduce_block", limit=8)(recv, gain)
     blocks = exchange(block)

time: 99.6 us -> 102 us (1.024)
  local copies, waits for them, and re-layouts: 0.11 us -> 2.31 us
  waiting for transfers between devices: 12.9 us -> 11.3 us
  blocking collectives: 29.6 us -> 31.2 us
    unnamed x4 -> x8, local copies, waits for them, and re-layouts: 0.01 us -> 2.21 us
    all_to_all x3, waiting for transfers between devices: 12.9 us -> 11.3 us  [exchange(): return lax.all_to_all(x, 'tiles', split_axis=0, concat_axis=0, tiled=True)]
    all_to_all x1, blocking collectives: 29.6 us -> 31.2 us  [exchange(): return lax.all_to_all(x, 'tiles', split_axis=0, concat_axis=0, tiled=True)]
where the time goes in v7:
time: 102 us; the launch traced here: 101 us
  Pallas kernels  31.9 us (31%)
  blocking collectives  31.2 us (31%)
  starting transfers between devices  23.1 us (23%)
  waiting for transfers between devices  11.3 us (11%)
  local copies, waits for them, and re-layouts  2.31 us (2%)
  between operations  1.42 us (1%)
    all_to_all x1, blocking collectives, exchange(): return lax.all_to_all(x, 'tiles', split_axis=0, concat_axis=0, tiled=True)  31.2 us
    all_to_all x3, starting transfers between devices, exchange(): return lax.all_to_all(x, 'tiles', split_axis=0, concat_axis=0, tiled=True)  23.1 us
    pallas_call x1, Pallas kernels, shards(): call(adjoint_kernel, (sds((SLOTS, CHAN), bf16), sds((32, 4, 4, 8, 128), b...  17.8 us
    all_to_all x3, waiting for transfers between devices, exchange(): return lax.all_to_all(x, 'tiles', split_axis=0, concat_axis=0, tiled=True)  11.3 us
    pallas_call x1, Pallas kernels, shards(): call(gather_feat, (sds((SLOTS, FEAT), bf16), sds((16, 128), jnp.int32)),...  5.6 us
    pallas_call x1, Pallas kernels, shards(): call(scatter_rows, sds((ROWS, FEAT), bf16), 2, scratch=[pltpu.VMEM((SLOTS...  4.21 us
    unnamed x8, local copies, waits for them, and re-layouts  2.21 us
  transfers between devices with their start and end apart: 3, of which 3 were waited for; matrix products, arithmetic and copies ran while one was open for 0% of the time, Pallas kernels for 27%

profile of v7, /device:TPU:1, one launch (start us, length us, event | category | flops | bytes accessed | tf_op | source)
XLA Modules:
  0.0 101.3 jit_solution(7911366529317005203)
XLA Ops:
  0.6 1.7 %gather_pos.1 = f32[128,128]{1,0:T(8,128)} custom-call(s32[16,128]{1,0:T(8,128)} %bitcast.23, s32[1,128]{1,0:T(1,128)} %count_hbm.1, f32[3,2048]{1,0:T(4,128)} %coords_hbm.1), custom_call_target="tpu_custom_call" | custom-call | tf_op jit(solution)/shard_map/gather_pos/pallas_call | solution.py:236
  2.4 11.5 %all-to-all-start = ((f32[128,1,128]{2,1,0:T(1,128)}), f32[128,1,128]{2,1,0:T(1,128)S(1)}, u32[]{:S(2)}, u32[]{:S(2)}) async-start(f32[128,1,128]{2,1,0:T(1,128)} %bitcast.22), calls=%async_computation | async-start | bytes 131072 | tf_op jit(solution)/shard_map/all_to_all | solution.py:230
  14.6 0.1 fusion.2
  14.6 0.1 fusion
  14.7 5.6 %gather_feat.1 = (bf16[2048,256]{1,0:T(8,128)(2,1)}, s32[16,128]{1,0:T(8,128)}) custom-call(s32[16,128]{1,0:T(8,128)} %bitcast.24, bf16[2048,256]{1,0:T(8,128)(2,1)} %feat_hbm.1), custom_call_target="tpu_custom_call" | custom-call | flops 4000000000 | bytes 2097152 | tf_op jit(solution)/shard_map/gather_feat/pallas_call | solution.py:248
  20.3 0.0 copy-start.2
  20.3 0.1 copy.11.trig_ref
  20.4 2.8 %all-to-all-done = f32[128,1,128]{2,1,0:T(1,128)S(1)} async-done(((f32[128,1,128]{2,1,0:T(1,128)}), f32[128,1,128]{2,1,0:T(1,128)S(1)}, u32[]{:S(2)}, u32[]{:S(2)}) %all-to-all-start) | async-done | bytes 65568 | tf_op jit(solution)/shard_map/all_to_all | solution.py:230
  23.2 7.0 %all-to-all-start.1 = ((bf16[128,16,256]{2,1,0:T(8,128)(2,1)}), bf16[128,16,256]{2,1,0:T(8,128)(2,1)S(1)}, u32[]{:S(2)}, u32[]{:S(2)}) async-start(bf16[128,16,256]{2,1,0:T(8,128)(2,1)} %bitcast.21), calls=%async_computation.1 | async-start | bytes 2097152 | tf_op jit(solution)/shard_map/all_to_all | solution.py:230
  30.2 0.0 copy-done.2
  30.2 17.8 %adjoint.1 = (bf16[2048,512]{1,0:T(8,128)(2,1)S(1)}, bf16[32,4,4,8,128]{4,3,2,1,0:T(8,128)(2,1)S(1)}, f32[1,512]{1,0:T(1,128)S(1)}) custom-call(f32[128,128]{1,0:T(8,128)S(1)} %bitcast.20, f32[64,4]{1,0:T(8,128)S(1)} %copy.11.trig_ref, bf16[4096,512]{1,0:T(8,128)(2,1)} %cot_hbm.1, bf16[256,512]{1,0:T(8,128)(2,1)S(1)} %copy-done.2), custom_call_target="tpu_custom_call" | custom-call | flops 20000000000 | bytes 8388608 | tf_op jit(solution)/shard_map/adjoint/pallas_call | solution.py:261
  48.0 0.0 copy-start
  48.0 1.0 copy-done
  49.0 0.3 all-to-all-done.1
  49.3 0.0 copy-start.1
  49.3 1.2 %copy-done.1 = bf16[32,4,4,8,128]{4,3,2,1,0:T(8,128)(2,1)S(1)} copy-done((bf16[32,4,4,8,128]{4,3,2,1,0:T(8,128)(2,1)S(1)}, bf16[32,4,4,8,128]{4,3,2,1,0:T(8,128)(2,1)}, u32[]{:S(2)}) %copy-start.1) | copy-done | bytes 1048600
  50.6 0.7 finish_tile.1
  51.3 0.0 copy-start.3
  51.3 31.2 %all_to_all.20.recv_ref = bf16[128,5,8,128]{3,2,1,0:T(8,128)(2,1)S(1)} all-to-all(bf16[128,5,8,128]{3,2,1,0:T(8,128)(2,1)S(1)} %bitcast.17), channel_id=1, replica_groups=mesh['tiles'=128] {'tiles'}, dimensions={0} | all-to-all | bytes 2621440 | tf_op jit(solution)/shard_map/all_to_all | solution.py:230
  82.5 0.9 reduce_block.1
  83.4 4.6 %all-to-all-start.3 = ((bf16[128,3,4,128]{3,2,1,0:T(4,128)(2,1)}), bf16[128,3,4,128]{3,2,1,0:T(4,128)(2,1)S(1)}, u32[]{:S(2)}, u32[]{:S(2)}) async-start(bf16[128,3,4,128]{3,2,1,0:T(4,128)(2,1)} %reduce_block.1), calls=%async_computation.3 | async-start | bytes 786432 | tf_op jit(solution)/shard_map/all_to_all | solution.py:230
  88.1 0.0 copy-done.3
  88.1 4.2 %scatter_rows.1 = bf16[2048,256]{1,0:T(8,128)(2,1)} custom-call(s32[16,128]{1,0:T(8,128)S(1)} %copy-done.3, bf16[128,5,8,128]{3,2,1,0:T(8,128)(2,1)S(1)} %all_to_all.20.recv_ref), custom_call_target="tpu_custom_call" | custom-call | flops 4000000000 | bytes 3145728 | tf_op jit(solution)/shard_map/scatter_rows/pallas_call | solution.py:292
  92.3 8.1 %all-to-all-done.3 = bf16[128,3,4,128]{3,2,1,0:T(4,128)(2,1)S(1)} async-done(((bf16[128,3,4,128]{3,2,1,0:T(4,128)(2,1)}), bf16[128,3,4,128]{3,2,1,0:T(4,128)(2,1)S(1)}, u32[]{:S(2)}, u32[]{:S(2)}) %all-to-all-start.3) | async-done | bytes 393248 | tf_op jit(solution)/shard_map/all_to_all | solution.py:230
  100.4 0.9 assemble.1
  (1 shorter events, 0.0 us)
Async XLA Ops:
  2.4 20.8 %all-to-all-start = ((f32[128,1,128]{2,1,0:T(1,128)}), f32[128,1,128]{2,1,0:T(1,128)S(1)}, u32[]{:S(2)}, u32[]{:S(2)}) async-start(f32[128,1,128]{2,1,0:T(1,128)} %bitcast.22), calls=%async_computation | async-start | bytes 131072 | tf_op jit(solution)/shard_map/all_to_all | solution.py:230
  20.3 9.9 %copy-start.2 = (bf16[256,512]{1,0:T(8,128)(2,1)S(1)}, bf16[256,512]{1,0:T(8,128)(2,1)}, u32[]{:S(2)}) copy-start(bf16[256,512]{1,0:T(8,128)(2,1)} %proj_hbm.1) | copy-start | bytes 786436
  23.2 26.1 %all-to-all-start.1 = ((bf16[128,16,256]{2,1,0:T(8,128)(2,1)}), bf16[128,16,256]{2,1,0:T(8,128)(2,1)S(1)}, u32[]{:S(2)}, u32[]{:S(2)}) async-start(bf16[128,16,256]{2,1,0:T(8,128)(2,1)} %bitcast.21), calls=%async_computation.1 | async-start | bytes 2097152 | tf_op jit(solution)/shard_map/all_to_all | solution.py:230
  48.0 1.0 copy-start
  49.3 1.2 %copy-start.1 = (bf16[32,4,4,8,128]{4,3,2,1,0:T(8,128)(2,1)S(1)}, bf16[32,4,4,8,128]{4,3,2,1,0:T(8,128)(2,1)}, u32[]{:S(2)}) copy-start(bf16[32,4,4,8,128]{4,3,2,1,0:T(8,128)(2,1)} %copy-done) | copy-start | bytes 3145732
  51.3 36.8 %copy-start.3 = (s32[16,128]{1,0:T(8,128)S(1)}, s32[16,128]{1,0:T(8,128)}, u32[]{:S(2)}) copy-start(s32[16,128]{1,0:T(8,128)} %get-tuple-element.12.rl_ref) | copy-start | bytes 24580
  83.4 17.0 %all-to-all-start.3 = ((bf16[128,3,4,128]{3,2,1,0:T(4,128)(2,1)}), bf16[128,3,4,128]{3,2,1,0:T(4,128)(2,1)S(1)}, u32[]{:S(2)}, u32[]{:S(2)}) async-start(bf16[128,3,4,128]{3,2,1,0:T(4,128)(2,1)} %reduce_block.1), calls=%async_computation.3 | async-start | bytes 786432 | tf_op jit(solution)/shard_map/all_to_all | solution.py:230

commit v8 on v6

--- a/solution.py
+++ b/solution.py
@@ -22,13 +22,13 @@
 DMA = pltpu.SemaphoreType.DMA
 
 
-def call(body, out_shape, n_in, scratch=(), in_specs=None, name=None, limit=24, cost=None):
+def call(body, out_shape, n_in, scratch=(), in_specs=None, out_specs=None, name=None, limit=24, cost=None):
     many = isinstance(out_shape, (tuple, list))
     return pl.pallas_call(
         body,
         out_shape=out_shape,
         in_specs=in_specs or [VM] * n_in,
-        out_specs=tuple(VM for _ in out_shape) if many else VM,
+        out_specs=out_specs or (tuple(VM for _ in out_shape) if many else VM),
         scratch_shapes=list(scratch),
         compiler_params=pltpu.CompilerParams(vmem_limit_bytes=int(limit * 1024 * 1024)),
         name=name,
@@ -70,26 +70,30 @@
     out_ref[...] = jnp.concatenate(pos + [jnp.zeros((80, 128), f32)], axis=0).T
 
 
-def gather_feat(rows_hbm, feat_hbm, out_ref, rl_ref, hot_ref, rows_ref, feat_ref, sems):
+def gather_feat(rows_hbm, feat_hbm, out_hbm, rl_ref, hot_ref, rows_ref, feat_ref, got_ref, sems):
     loads = load_all([(rows_hbm, rows_ref), (feat_hbm, feat_ref)], sems)
     loads[0].wait()
     x = jnp.concatenate([rows_ref[...].astype(f32), jnp.zeros((112, 128), f32)], axis=0).T
     rl = slot_major(x[:, 0:16])
     rl_ref[...] = rl.astype(jnp.int32)
-    lane = lax.broadcasted_iota(jnp.int32, (128, 128), 1)
+    lane = lax.broadcasted_iota(jnp.int32, (128, 128), 1).astype(jnp.int16)
+    stores = []
     for b in range(4):
         for q in range(4):
             r = 4 * b + q
-            col = jnp.broadcast_to(rl[r : r + 1, :], (128, 128)).T.astype(jnp.int32)
+            col = jnp.broadcast_to(rl[r : r + 1, :], (128, 128)).T.astype(jnp.int32).astype(jnp.int16)
             for t in range(ROWS // 128):
-                hot_ref[128 * q : 128 * q + 128, 128 * t : 128 * t + 128] = jnp.where(
-                    col == lane + 128 * t, 1.0, 0.0
-                ).astype(bf16)
+                hot_ref[b, 128 * q : 128 * q + 128, 128 * t : 128 * t + 128] = jnp.where(
+                    col == lane + jnp.int16(128 * t), jnp.ones((), bf16), jnp.zeros((), bf16)
+                )
         if b == 0:
             loads[1].wait()
-        out_ref[512 * b : 512 * b + 512, :] = jnp.dot(
-            hot_ref[...], feat_ref[...], preferred_element_type=f32
-        ).astype(bf16)
+        part = slice(512 * b, 512 * b + 512)
+        got_ref[part] = jnp.dot(hot_ref[b], feat_ref[...], preferred_element_type=f32).astype(bf16)
+        stores.append(pltpu.make_async_copy(got_ref.at[part], out_hbm.at[part], sems.at[2 + b]))
+        stores[b].start()
+    for c in stores:
+        c.wait()
 
 
 def adjoint_kernel(
@@ -248,7 +252,14 @@
         (sds((SLOTS, FEAT), bf16), sds((16, 128), jnp.int32)),
         2,
         in_specs=[HBM] * 2,
-        scratch=[pltpu.VMEM((512, ROWS), bf16), pltpu.VMEM((CAP, N_DEV), jnp.int32), pltpu.VMEM((ROWS, FEAT), bf16), DMA((2,))],
+        out_specs=(HBM, VM),
+        scratch=[
+            pltpu.VMEM((4, 512, ROWS), bf16),
+            pltpu.VMEM((CAP, N_DEV), jnp.int32),
+            pltpu.VMEM((ROWS, FEAT), bf16),
+            pltpu.VMEM((SLOTS, FEAT), bf16),
+            DMA((6,)),
+        ],
         name="gather_feat",
         limit=59,
         cost=cost(4 * 10**9, 2 * 2**20),

time: 99.6 us -> 99.1 us (level)
  no operation moved by 1% of the time
where the time goes in v8:
time: 99.1 us; the launch traced here: 98.8 us
  Pallas kernels  31.6 us (32%)
  blocking collectives  29.5 us (30%)
  starting transfers between devices  22.6 us (23%)
  waiting for transfers between devices  13.3 us (13%)
  between operations  1.4 us (1%)
    all_to_all x1, blocking collectives, exchange(): return lax.all_to_all(x, 'tiles', split_axis=0, concat_axis=0, tiled=True)  29.5 us
    all_to_all x3, starting transfers between devices, exchange(): return lax.all_to_all(x, 'tiles', split_axis=0, concat_axis=0, tiled=True)  22.6 us
    pallas_call x1, Pallas kernels, shards(): call(adjoint_kernel, (sds((SLOTS, CHAN), bf16), sds((1, CHAN), f32)), 3,...  17.2 us
    all_to_all x3, waiting for transfers between devices, exchange(): return lax.all_to_all(x, 'tiles', split_axis=0, concat_axis=0, tiled=True)  13.3 us
    pallas_call x1, Pallas kernels, shards(): call(gather_feat, (sds((SLOTS, FEAT), bf16), sds((16, 128), jnp.int32)),...  5.15 us
    pallas_call x1, Pallas kernels, shards(): call(scatter_rows, sds((ROWS, FEAT), bf16), 2, scratch=[pltpu.VMEM((SLOTS...  4.2 us
  transfers between devices with their start and end apart: 3, of which 3 were waited for; matrix products, arithmetic and copies ran while one was open for 0% of the time, Pallas kernels for 27%

profile of v8, /device:TPU:1, one launch (start us, length us, event | category | flops | bytes accessed | tf_op | source)
XLA Modules:
  0.0 98.8 jit_solution(12726655880602239883)
XLA Ops:
  0.6 1.7 %gather_pos.1 = f32[128,128]{1,0:T(8,128)} custom-call(s32[16,128]{1,0:T(8,128)} %bitcast.23, s32[1,128]{1,0:T(1,128)} %count_hbm.1, f32[3,2048]{1,0:T(4,128)} %coords_hbm.1), custom_call_target="tpu_custom_call" | custom-call | tf_op jit(solution)/shard_map/gather_pos/pallas_call | solution.py:238
  2.4 11.5 %all-to-all-start = ((f32[128,1,128]{2,1,0:T(1,128)}), f32[128,1,128]{2,1,0:T(1,128)S(1)}, u32[]{:S(2)}, u32[]{:S(2)}) async-start(f32[128,1,128]{2,1,0:T(1,128)} %bitcast.22), calls=%async_computation | async-start | bytes 131072 | tf_op jit(solution)/shard_map/all_to_all | solution.py:232
  14.6 0.1 fusion.2
  14.6 0.1 fusion
  14.7 5.2 %gather_feat.1 = (bf16[2048,256]{1,0:T(8,128)(2,1)}, s32[16,128]{1,0:T(8,128)}) custom-call(s32[16,128]{1,0:T(8,128)} %bitcast.24, bf16[2048,256]{1,0:T(8,128)(2,1)} %feat_hbm.1), custom_call_target="tpu_custom_call" | custom-call | flops 4000000000 | bytes 2097152 | tf_op jit(solution)/shard_map/gather_feat/pallas_call | solution.py:250
  19.8 0.1 copy.11.trig_ref
  19.9 3.3 %all-to-all-done = f32[128,1,128]{2,1,0:T(1,128)S(1)} async-done(((f32[128,1,128]{2,1,0:T(1,128)}), f32[128,1,128]{2,1,0:T(1,128)S(1)}, u32[]{:S(2)}, u32[]{:S(2)}) %all-to-all-start) | async-done | bytes 65568 | tf_op jit(solution)/shard_map/all_to_all | solution.py:232
  23.2 6.5 %all-to-all-start.1 = ((bf16[128,16,256]{2,1,0:T(8,128)(2,1)}), bf16[128,16,256]{2,1,0:T(8,128)(2,1)S(1)}, u32[]{:S(2)}, u32[]{:S(2)}) async-start(bf16[128,16,256]{2,1,0:T(8,128)(2,1)} %bitcast.21), calls=%async_computation.1 | async-start | bytes 2097152 | tf_op jit(solution)/shard_map/all_to_all | solution.py:232
  29.7 0.0 copy-start
  29.7 17.2 %adjoint.1 = (bf16[2048,512]{1,0:T(8,128)(2,1)S(1)}, f32[1,512]{1,0:T(1,128)S(1)}) custom-call(f32[128,128]{1,0:T(8,128)S(1)} %bitcast.20, f32[64,4]{1,0:T(8,128)S(1)} %copy.11.trig_ref, bf16[4096,512]{1,0:T(8,128)(2,1)} %cot_hbm.1), custom_call_target="tpu_custom_call" | custom-call | flops 20000000000 | bytes 8388608 | tf_op jit(solution)/shard_map/adjoint/pallas_call | solution.py:270
  46.9 2.0 %all-to-all-done.1 = bf16[128,16,256]{2,1,0:T(8,128)(2,1)S(1)} async-done(((bf16[128,16,256]{2,1,0:T(8,128)(2,1)}), bf16[128,16,256]{2,1,0:T(8,128)(2,1)S(1)}, u32[]{:S(2)}, u32[]{:S(2)}) %all-to-all-start.1) | async-done | bytes 1048608 | tf_op jit(solution)/shard_map/all_to_all | solution.py:232
  48.9 0.0 copy-done
  48.9 1.5 %finish_tile.1 = bf16[32,4,5,8,128]{4,3,2,1,0:T(8,128)(2,1)S(1)} custom-call(bf16[2048,512]{1,0:T(8,128)(2,1)S(1)} %get-tuple-element.14.adj_ref, bf16[2048,256]{1,0:T(8,128)(2,1)S(1)} %bitcast.18, bf16[256,512]{1,0:T(8,128)(2,1)S(1)} %copy-done), custom_call_target="tpu_custom_call" | custom-call | tf_op jit(solution)/shard_map/finish_tile/pallas_call | solution.py:290
  50.4 0.0 copy-start.1
  50.4 29.5 %all_to_all.20.recv_ref = bf16[128,5,8,128]{3,2,1,0:T(8,128)(2,1)S(1)} all-to-all(bf16[128,5,8,128]{3,2,1,0:T(8,128)(2,1)S(1)} %bitcast.17), channel_id=1, replica_groups=mesh['tiles'=128] {'tiles'}, dimensions={0} | all-to-all | bytes 2621440 | tf_op jit(solution)/shard_map/all_to_all | solution.py:232
  80.0 0.9 reduce_block.1
  80.9 4.6 %all-to-all-start.3 = ((bf16[128,3,4,128]{3,2,1,0:T(4,128)(2,1)}), bf16[128,3,4,128]{3,2,1,0:T(4,128)(2,1)S(1)}, u32[]{:S(2)}, u32[]{:S(2)}) async-start(bf16[128,3,4,128]{3,2,1,0:T(4,128)(2,1)} %reduce_block.1), calls=%async_computation.3 | async-start | bytes 786432 | tf_op jit(solution)/shard_map/all_to_all | solution.py:232
  85.6 0.0 copy-done.1
  85.6 4.2 %scatter_rows.1 = bf16[2048,256]{1,0:T(8,128)(2,1)} custom-call(s32[16,128]{1,0:T(8,128)S(1)} %copy-done.1, bf16[128,5,8,128]{3,2,1,0:T(8,128)(2,1)S(1)} %all_to_all.20.recv_ref), custom_call_target="tpu_custom_call" | custom-call | flops 4000000000 | bytes 3145728 | tf_op jit(solution)/shard_map/scatter_rows/pallas_call | solution.py:302
  89.8 8.1 %all-to-all-done.3 = bf16[128,3,4,128]{3,2,1,0:T(4,128)(2,1)S(1)} async-done(((bf16[128,3,4,128]{3,2,1,0:T(4,128)(2,1)}), bf16[128,3,4,128]{3,2,1,0:T(4,128)(2,1)S(1)}, u32[]{:S(2)}, u32[]{:S(2)}) %all-to-all-start.3) | async-done | bytes 393248 | tf_op jit(solution)/shard_map/all_to_all | solution.py:232
  97.9 0.9 assemble.1
  (1 shorter events, 0.0 us)
Async XLA Ops:
  2.4 20.8 %all-to-all-start = ((f32[128,1,128]{2,1,0:T(1,128)}), f32[128,1,128]{2,1,0:T(1,128)S(1)}, u32[]{:S(2)}, u32[]{:S(2)}) async-start(f32[128,1,128]{2,1,0:T(1,128)} %bitcast.22), calls=%async_computation | async-start | bytes 131072 | tf_op jit(solution)/shard_map/all_to_all | solution.py:232
  23.2 25.7 %all-to-all-start.1 = ((bf16[128,16,256]{2,1,0:T(8,128)(2,1)}), bf16[128,16,256]{2,1,0:T(8,128)(2,1)S(1)}, u32[]{:S(2)}, u32[]{:S(2)}) async-start(bf16[128,16,256]{2,1,0:T(8,128)(2,1)} %bitcast.21), calls=%async_computation.1 | async-start | bytes 2097152 | tf_op jit(solution)/shard_map/all_to_all | solution.py:232
  29.7 19.2 %copy-start = (bf16[256,512]{1,0:T(8,128)(2,1)S(1)}, bf16[256,512]{1,0:T(8,128)(2,1)}, u32[]{:S(2)}) copy-start(bf16[256,512]{1,0:T(8,128)(2,1)} %proj_hbm.1) | copy-start | bytes 786436
  50.4 35.2 %copy-start.1 = (s32[16,128]{1,0:T(8,128)S(1)}, s32[16,128]{1,0:T(8,128)}, u32[]{:S(2)}) copy-start(s32[16,128]{1,0:T(8,128)} %get-tuple-element.11.rl_ref) | copy-start | bytes 24580
  80.9 17.0 %all-to-all-start.3 = ((bf16[128,3,4,128]{3,2,1,0:T(4,128)(2,1)}), bf16[128,3,4,128]{3,2,1,0:T(4,128)(2,1)S(1)}, u32[]{:S(2)}, u32[]{:S(2)}) async-start(bf16[128,3,4,128]{3,2,1,0:T(4,128)(2,1)} %reduce_block.1), calls=%async_computation.3 | async-start | bytes 786432 | tf_op jit(solution)/shard_map/all_to_all | solution.py:232

commit v9 on v8

--- a/solution.py
+++ b/solution.py
@@ -164,14 +164,9 @@
             weigh(7 * 512 + 128 * m, q, sc, lg)
     gain_ref[...] = jnp.sum(gacc_ref[...], axis=0, keepdims=True) * (1.0 / 2048.0)
 
-    def slots(n, _):
-        rs = pl.ds(pl.multiple_of(n * 1024, 1024), 1024)
-        adj_ref[rs, :] = lax.dot_general(
-            k_ref[:, rs], w_ref[...], (((0,), (0,)), ((), ())), preferred_element_type=f32
-        ).astype(bf16)
-        return 0
-
-    lax.fori_loop(0, SLOTS // 1024, slots, 0)
+    adj_ref[...] = lax.dot_general(
+        k_ref[...], w_ref[...], (((0,), (0,)), ((), ())), preferred_element_type=f32
+    ).astype(bf16)
 
 
 def finish_tile(adj_ref, feat_ref, proj_hbm, out_ref, proj_ref, sems):
@@ -191,7 +186,7 @@
 
 
 def reduce_block(recv_ref, gain_ref, out_ref):
-    total = jnp.sum(recv_ref[:, 4].astype(f32), axis=0)
+    total = jnp.sum(jnp.sum(recv_ref[:, 4].astype(f32).reshape(16, 8, 8, 128), axis=0), axis=0)
     g = [gain_ref[:, 128 * i : 128 * i + 128] for i in range(4)]
     block = jnp.concatenate([total] + g, axis=0).reshape(3, 4, 128).astype(bf16)
     out_ref[...] = jnp.broadcast_to(block[None], (N_DEV, 3, 4, 128))

time: 99.1 us -> 98.8 us (level)
  no operation moved by 1% of the time
where the time goes in v9:
time: 98.8 us; the launch traced here: 98.4 us
  Pallas kernels  31.3 us (32%)
  blocking collectives  29.3 us (30%)
  starting transfers between devices  22.6 us (23%)
  waiting for transfers between devices  13.6 us (14%)
  between operations  1.4 us (1%)
    all_to_all x1, blocking collectives, exchange(): return lax.all_to_all(x, 'tiles', split_axis=0, concat_axis=0, tiled=True)  29.3 us
    all_to_all x3, starting transfers between devices, exchange(): return lax.all_to_all(x, 'tiles', split_axis=0, concat_axis=0, tiled=True)  22.6 us
    pallas_call x1, Pallas kernels, shards(): call(adjoint_kernel, (sds((SLOTS, CHAN), bf16), sds((1, CHAN), f32)), 3,...  16.9 us
    all_to_all x3, waiting for transfers between devices, exchange(): return lax.all_to_all(x, 'tiles', split_axis=0, concat_axis=0, tiled=True)  13.6 us
    pallas_call x1, Pallas kernels, shards(): call(gather_feat, (sds((SLOTS, FEAT), bf16), sds((16, 128), jnp.int32)),...  5.15 us
    pallas_call x1, Pallas kernels, shards(): call(scatter_rows, sds((ROWS, FEAT), bf16), 2, scratch=[pltpu.VMEM((SLOTS...  4.21 us
  transfers between devices with their start and end apart: 3, of which 3 were waited for; matrix products, arithmetic and copies ran while one was open for 0% of the time, Pallas kernels for 27%

profile of v9, /device:TPU:1, one launch (start us, length us, event | category | flops | bytes accessed | tf_op | source)
XLA Modules:
  0.0 98.4 jit_solution(15607642428477358324)
XLA Ops:
  0.6 1.7 %gather_pos.1 = f32[128,128]{1,0:T(8,128)} custom-call(s32[16,128]{1,0:T(8,128)} %bitcast.23, s32[1,128]{1,0:T(1,128)} %count_hbm.1, f32[3,2048]{1,0:T(4,128)} %coords_hbm.1), custom_call_target="tpu_custom_call" | custom-call | tf_op jit(solution)/shard_map/gather_pos/pallas_call | solution.py:233
  2.4 11.5 %all-to-all-start = ((f32[128,1,128]{2,1,0:T(1,128)}), f32[128,1,128]{2,1,0:T(1,128)S(1)}, u32[]{:S(2)}, u32[]{:S(2)}) async-start(f32[128,1,128]{2,1,0:T(1,128)} %bitcast.22), calls=%async_computation | async-start | bytes 131072 | tf_op jit(solution)/shard_map/all_to_all | solution.py:227
  14.6 0.1 fusion.2
  14.6 0.1 fusion
  14.7 5.2 %gather_feat.1 = (bf16[2048,256]{1,0:T(8,128)(2,1)}, s32[16,128]{1,0:T(8,128)}) custom-call(s32[16,128]{1,0:T(8,128)} %bitcast.24, bf16[2048,256]{1,0:T(8,128)(2,1)} %feat_hbm.1), custom_call_target="tpu_custom_call" | custom-call | flops 4000000000 | bytes 2097152 | tf_op jit(solution)/shard_map/gather_feat/pallas_call | solution.py:245
  19.8 0.1 copy.11.trig_ref
  19.9 3.3 %all-to-all-done = f32[128,1,128]{2,1,0:T(1,128)S(1)} async-done(((f32[128,1,128]{2,1,0:T(1,128)}), f32[128,1,128]{2,1,0:T(1,128)S(1)}, u32[]{:S(2)}, u32[]{:S(2)}) %all-to-all-start) | async-done | bytes 65568 | tf_op jit(solution)/shard_map/all_to_all | solution.py:227
  23.2 6.5 %all-to-all-start.1 = ((bf16[128,16,256]{2,1,0:T(8,128)(2,1)}), bf16[128,16,256]{2,1,0:T(8,128)(2,1)S(1)}, u32[]{:S(2)}, u32[]{:S(2)}) async-start(bf16[128,16,256]{2,1,0:T(8,128)(2,1)} %bitcast.21), calls=%async_computation.1 | async-start | bytes 2097152 | tf_op jit(solution)/shard_map/all_to_all | solution.py:227
  29.7 0.0 copy-start
  29.7 16.9 %adjoint.1 = (bf16[2048,512]{1,0:T(8,128)(2,1)S(1)}, f32[1,512]{1,0:T(1,128)S(1)}) custom-call(f32[128,128]{1,0:T(8,128)S(1)} %bitcast.20, f32[64,4]{1,0:T(8,128)S(1)} %copy.11.trig_ref, bf16[4096,512]{1,0:T(8,128)(2,1)} %cot_hbm.1), custom_call_target="tpu_custom_call" | custom-call | flops 20000000000 | bytes 8388608 | tf_op jit(solution)/shard_map/adjoint/pallas_call | solution.py:265
  46.7 2.2 %all-to-all-done.1 = bf16[128,16,256]{2,1,0:T(8,128)(2,1)S(1)} async-done(((bf16[128,16,256]{2,1,0:T(8,128)(2,1)}), bf16[128,16,256]{2,1,0:T(8,128)(2,1)S(1)}, u32[]{:S(2)}, u32[]{:S(2)}) %all-to-all-start.1) | async-done | bytes 1048608 | tf_op jit(solution)/shard_map/all_to_all | solution.py:227
  48.9 0.0 copy-done
  48.9 1.5 %finish_tile.1 = bf16[32,4,5,8,128]{4,3,2,1,0:T(8,128)(2,1)S(1)} custom-call(bf16[2048,512]{1,0:T(8,128)(2,1)S(1)} %get-tuple-element.14.adj_ref, bf16[2048,256]{1,0:T(8,128)(2,1)S(1)} %bitcast.18, bf16[256,512]{1,0:T(8,128)(2,1)S(1)} %copy-done), custom_call_target="tpu_custom_call" | custom-call | tf_op jit(solution)/shard_map/finish_tile/pallas_call | solution.py:285
  50.4 0.0 copy-start.1
  50.4 29.3 %all_to_all.20.recv_ref = bf16[128,5,8,128]{3,2,1,0:T(8,128)(2,1)S(1)} all-to-all(bf16[128,5,8,128]{3,2,1,0:T(8,128)(2,1)S(1)} %bitcast.17), channel_id=1, replica_groups=mesh['tiles'=128] {'tiles'}, dimensions={0} | all-to-all | bytes 2621440 | tf_op jit(solution)/shard_map/all_to_all | solution.py:227
  79.7 0.9 reduce_block.1
  80.6 4.6 %all-to-all-start.3 = ((bf16[128,3,4,128]{3,2,1,0:T(4,128)(2,1)}), bf16[128,3,4,128]{3,2,1,0:T(4,128)(2,1)S(1)}, u32[]{:S(2)}, u32[]{:S(2)}) async-start(bf16[128,3,4,128]{3,2,1,0:T(4,128)(2,1)} %reduce_block.1), calls=%async_computation.3 | async-start | bytes 786432 | tf_op jit(solution)/shard_map/all_to_all | solution.py:227
  85.2 0.0 copy-done.1
  85.2 4.2 %scatter_rows.1 = bf16[2048,256]{1,0:T(8,128)(2,1)} custom-call(s32[16,128]{1,0:T(8,128)S(1)} %copy-done.1, bf16[128,5,8,128]{3,2,1,0:T(8,128)(2,1)S(1)} %all_to_all.20.recv_ref), custom_call_target="tpu_custom_call" | custom-call | flops 4000000000 | bytes 3145728 | tf_op jit(solution)/shard_map/scatter_rows/pallas_call | solution.py:297
  89.4 8.1 %all-to-all-done.3 = bf16[128,3,4,128]{3,2,1,0:T(4,128)(2,1)S(1)} async-done(((bf16[128,3,4,128]{3,2,1,0:T(4,128)(2,1)}), bf16[128,3,4,128]{3,2,1,0:T(4,128)(2,1)S(1)}, u32[]{:S(2)}, u32[]{:S(2)}) %all-to-all-start.3) | async-done | bytes 393248 | tf_op jit(solution)/shard_map/all_to_all | solution.py:227
  97.6 0.9 assemble.1
  (1 shorter events, 0.0 us)
Async XLA Ops:
  2.4 20.8 %all-to-all-start = ((f32[128,1,128]{2,1,0:T(1,128)}), f32[128,1,128]{2,1,0:T(1,128)S(1)}, u32[]{:S(2)}, u32[]{:S(2)}) async-start(f32[128,1,128]{2,1,0:T(1,128)} %bitcast.22), calls=%async_computation | async-start | bytes 131072 | tf_op jit(solution)/shard_map/all_to_all | solution.py:227
  23.2 25.7 %all-to-all-start.1 = ((bf16[128,16,256]{2,1,0:T(8,128)(2,1)}), bf16[128,16,256]{2,1,0:T(8,128)(2,1)S(1)}, u32[]{:S(2)}, u32[]{:S(2)}) async-start(bf16[128,16,256]{2,1,0:T(8,128)(2,1)} %bitcast.21), calls=%async_computation.1 | async-start | bytes 2097152 | tf_op jit(solution)/shard_map/all_to_all | solution.py:227
  29.7 19.2 %copy-start = (bf16[256,512]{1,0:T(8,128)(2,1)S(1)}, bf16[256,512]{1,0:T(8,128)(2,1)}, u32[]{:S(2)}) copy-start(bf16[256,512]{1,0:T(8,128)(2,1)} %proj_hbm.1) | copy-start | bytes 786436
  50.4 34.8 %copy-start.1 = (s32[16,128]{1,0:T(8,128)S(1)}, s32[16,128]{1,0:T(8,128)}, u32[]{:S(2)}) copy-start(s32[16,128]{1,0:T(8,128)} %get-tuple-element.11.rl_ref) | copy-start | bytes 24580
  80.6 17.0 %all-to-all-start.3 = ((bf16[128,3,4,128]{3,2,1,0:T(4,128)(2,1)}), bf16[128,3,4,128]{3,2,1,0:T(4,128)(2,1)S(1)}, u32[]{:S(2)}, u32[]{:S(2)}) async-start(bf16[128,3,4,128]{3,2,1,0:T(4,128)(2,1)} %reduce_block.1), calls=%async_computation.3 | async-start | bytes 786432 | tf_op jit(solution)/shard_map/all_to_all | solution.py:227
